TPU v7x, 32 devices: a whole 2x2x4 slice. The times are simulated.
32 devices in a mesh: inp: 2 (over y), hid: 4 (over x, core), tok: 4 (over z).
Axes of the slice: x: 2, y: 2, z: 4, core: 2. Of those that a mesh axis runs over, the one named last changes fastest.
Arguments:
- tokens: float32 [512, 3072], P(('tok', 'hid'), 'inp'), may hold values from -6 to 6
- targets: float32 [512, 3072], P(('tok', 'hid'), 'inp'), may hold values from -6 to 6
- sample_ids: int32 [512], P(('tok', 'hid')), may hold values from 0 to 15, never falling along the last dimension, each value on 1 to 64 neighbouring positions
- labels: int32 [16], replicated, may hold values from 0 to 1
- utility: float32 [16], replicated, may hold values from 0.5 to 4
- ref_loss: float32 [16], replicated, may hold values from 0.9 to 1.9
- w_in: float32 [3072, 6144], P(('inp', 'tok'), 'hid'), may hold values from -0.109375 to 0.109375
- w_out: float32 [6144, 3072], P(('hid', 'tok'), 'inp'), may hold values from -0.078125 to 0.078125
- m_in: float32 [3072, 6144], P(('inp', 'tok'), 'hid'), may hold values from -6 to 6
- m_out: float32 [6144, 3072], P(('hid', 'tok'), 'inp'), may hold values from -6 to 6
- v_in: float32 [3072, 6144], P(('inp', 'tok'), 'hid'), may hold values from 0.5 to 20
- v_out: float32 [6144, 3072], P(('hid', 'tok'), 'inp'), may hold values from 0.5 to 20
- e_in: float32 [3072, 6144], P(('inp', 'tok'), 'hid'), may hold values from -0.109375 to 0.109375
- e_out: float32 [6144, 3072], P(('hid', 'tok'), 'inp'), may hold values from -0.078125 to 0.078125
Outputs:
- loss: float32 [], replicated
- new_w_in: float32 [3072, 6144], P('inp', 'hid')
- new_w_out: float32 [6144, 3072], P('hid', 'inp')
- new_m_in: float32 [3072, 6144], P(('inp', 'tok'), 'hid')
- new_m_out: float32 [6144, 3072], P(('hid', 'tok'), 'inp')
- new_v_in: float32 [3072, 6144], P(('inp', 'tok'), 'hid')
- new_v_out: float32 [6144, 3072], P(('hid', 'tok'), 'inp')
- new_e_in: float32 [3072, 6144], P(('inp', 'tok'), 'hid')
- new_e_out: float32 [6144, 3072], P(('hid', 'tok'), 'inp')
Inputs may be any that keep to these rules, and one draw needn't show every extreme that they name: `sample_ids`: sample numbers never fall along the tokens; every sample has 1 to 64 tokens, one exactly that many.
All inputs are finite; a program needn't handle non-finite values.
Results may differ from a plain program's by a relative error of at most 0.00022.
Values sent between devices are 32-bit elements; how exact they have to be, the bound alone decides.
A program may use at most 128 MiB of HBM per device.

v0:
```python
import jax
import jax.numpy as jnp
from jax import lax
from jax.sharding import PartitionSpec as P

D = 3072
SAMPLES = 16


highest = lax.Precision.HIGHEST
gelu_c = 0.7978845608028654
gelu_k = 0.044715
kto_beta = 4.0
loss_scale = 1048576.0
beta_one = 0.9
beta_two = 0.95
adam_eps = 1e-08
learn_rate = 0.001
decay_rate = 0.1
ema_rate = 0.99
bias_one = 1.0 - 0.9**10
bias_two = 1.0 - 0.95**10


def gelu_parts(hidden):
    inner = gelu_c * (hidden + gelu_k * hidden * hidden * hidden)
    tangent = jnp.tanh(inner)
    active = 0.5 * hidden * (1.0 + tangent)
    slope = 0.5 * (1.0 + tangent) + 0.5 * hidden * (1.0 - tangent * tangent) * gelu_c * (
        1.0 + 3.0 * gelu_k * hidden * hidden
    )
    return (active, slope)


def adamw(weight, moment_one, moment_two, average, gradient):
    moment_one = beta_one * moment_one + (1.0 - beta_one) * gradient
    moment_two = beta_two * moment_two + (1.0 - beta_two) * gradient * gradient
    update = learn_rate * (moment_one / bias_one) / (jnp.sqrt(moment_two / bias_two) + adam_eps)
    weight = weight - update - learn_rate * decay_rate * weight
    average = ema_rate * average + (1.0 - ema_rate) * weight
    return (weight, moment_one, moment_two, average)


def kto_terms(sq_sums, counts, labels, utility, ref_loss):
    sample_loss = sq_sums / (counts * D)
    signs = 2.0 * labels.astype(jnp.float32) - 1.0
    chosen = jax.nn.sigmoid(signs * kto_beta * (ref_loss - sample_loss))
    loss = -jnp.sum(utility * chosen) / SAMPLES
    dloss = utility * chosen * (1.0 - chosen) * signs * kto_beta / SAMPLES
    sample_coef = loss_scale * 2.0 * dloss / (counts * D)
    return (loss, sample_coef)


def contract_rows(left, right):
    return lax.dot_general(left, right, (((0,), (0,)), ((), ())), precision=highest)


def on_device(
    tokens,
    targets,
    sample_ids,
    labels,
    utility,
    ref_loss,
    w_in,
    w_out,
    m_in,
    m_out,
    v_in,
    v_out,
    e_in,
    e_out,
):
    all_rows = lax.all_gather(tokens, "hid", axis=0, tiled=True)
    w_out_block = lax.all_gather(w_out, "tok", axis=0, tiled=True)
    hidden_part = jnp.dot(
        all_rows,
        lax.all_gather(w_in, "tok", axis=0, tiled=True),
        precision=highest,
        preferred_element_type=jnp.float32,
    )
    hidden_share = lax.psum_scatter(hidden_part, "inp", scatter_dimension=0, tiled=True)
    active_share, slope_share = gelu_parts(hidden_share)
    active = lax.all_gather(active_share, "inp", axis=0, tiled=True)
    picked = active
    output = lax.psum_scatter(
        jnp.dot(picked, w_out_block, precision=highest, preferred_element_type=jnp.float32),
        "hid",
        scatter_dimension=0,
        tiled=True,
    )
    error_rows = output - targets
    onehot = (sample_ids[:, None] == jnp.arange(SAMPLES, dtype=jnp.int32)[None, :]).astype(
        jnp.float32
    )
    token_sq = jnp.sum(error_rows * error_rows, axis=1)
    local_sq = jnp.dot(token_sq, onehot, precision=highest)
    leading = lax.axis_index("inp") == 0
    local_counts = jnp.sum(onehot, axis=0) * jnp.where(leading, 1.0, 0.0)
    sq_sums, counts = lax.psum((local_sq, local_counts), ("inp", "hid", "tok"))
    loss, sample_coef = kto_terms(sq_sums, counts, labels, utility, ref_loss)
    d_output = error_rows * jnp.dot(onehot, sample_coef, precision=highest)[:, None]
    d_all = lax.all_gather(d_output, "hid", axis=0, tiled=True)
    picked = active
    grad_out = lax.psum_scatter(
        contract_rows(picked, d_all), "tok", scatter_dimension=0, tiled=True
    )
    d_active = lax.dot_general(d_all, w_out_block, (((1,), (1,)), ((), ())), precision=highest)
    d_share = lax.psum_scatter(d_active, "inp", scatter_dimension=0, tiled=True) * slope_share
    d_hidden = lax.all_gather(d_share, "inp", axis=0, tiled=True)
    picked = all_rows
    grad_in = lax.psum_scatter(
        contract_rows(picked, d_hidden), "tok", scatter_dimension=0, tiled=True
    )
    weight_in, new_m_in, new_v_in, new_e_in = adamw(w_in, m_in, v_in, e_in, grad_in)
    weight_out, new_m_out, new_v_out, new_e_out = adamw(w_out, m_out, v_out, e_out, grad_out)
    new_w_in, new_w_out = (
        lax.all_gather(weight_in, "tok", axis=0, tiled=True),
        lax.all_gather(weight_out, "tok", axis=0, tiled=True),
    )
    return (
        loss,
        new_w_in,
        new_w_out,
        new_m_in,
        new_m_out,
        new_v_in,
        new_v_out,
        new_e_in,
        new_e_out,
    )


def solution(mesh):
    in_specs = (
        P(("tok", "hid"), "inp"),
        P(("tok", "hid"), "inp"),
        P(("tok", "hid")),
        P(),
        P(),
        P(),
        P(("inp", "tok"), "hid"),
        P(("hid", "tok"), "inp"),
        P(("inp", "tok"), "hid"),
        P(("hid", "tok"), "inp"),
        P(("inp", "tok"), "hid"),
        P(("hid", "tok"), "inp"),
        P(("inp", "tok"), "hid"),
        P(("hid", "tok"), "inp"),
    )
    out_specs = (
        P(),
        P("inp", "hid"),
        P("hid", "inp"),
        P(("inp", "tok"), "hid"),
        P(("hid", "tok"), "inp"),
        P(("inp", "tok"), "hid"),
        P(("hid", "tok"), "inp"),
        P(("inp", "tok"), "hid"),
        P(("hid", "tok"), "inp"),
    )
    return jax.shard_map(
        on_device, mesh=mesh, in_specs=in_specs, out_specs=out_specs, check_vma=False
    )
```

profile of v0, /device:TPU:0, one launch (start us, length us, event | category | flops | bytes accessed | tf_op | source)
XLA Modules:
  0.0 1165.6 jit_solution(14150017617340313414)
XLA Ops:
  7.2 0.0 all-gather.5.cloned.1.call-start
  7.2 0.7 all-gather.5.cloned.1.call-update
  7.9 0.0 reduce-scatter.6.cloned.1.call-start
  8.0 0.1 copy-done.11
  8.1 10.0 all_gather.24
  18.1 161.0 %all-gather.5.cloned.1.call-done = f32[1536,1536]{1,0:T(8,128)} async-done(((f32[384,1536]{1,0:T(8,128)}), f32[1536,1536]{1,0:T(8,128)}) %all-gather.5.cloned.1.call-update) | async-done | bytes 9437200 | tf_op jit(solution)/shard_map/all_gather | solution.py:78
  179.1 8.5 fusion.24
  187.6 0.0 reduce-scatter.6.cloned.1.call-update
  187.6 0.0 all-gather.7.cloned.1.call-start
  187.7 0.7 all-gather.7.cloned.1.call-update
  188.3 0.0 reduce-scatter.8.cloned.1.call-start
  188.4 15.0 %reduce-scatter.6.cloned.1.call-done = f32[64,1536]{1,0:T(8,128)} async-done(((f32[128,1536]{1,0:T(8,128)}), f32[64,1536]{1,0:T(8,128)}) %reduce-scatter.6.cloned.1.call-update) | async-done | bytes 393232 | tf_op jit(solution)/shard_map/reduce_scatter | solution.py:82
  203.4 1.1 add_multiply_fusion
  204.5 11.5 all_gather.26
  216.1 155.8 %all-gather.7.cloned.1.call-done = f32[1536,1536]{1,0:T(8,128)} async-done(((f32[384,1536]{1,0:T(8,128)}), f32[1536,1536]{1,0:T(8,128)}) %all-gather.7.cloned.1.call-update) | async-done | bytes 9437200 | tf_op jit(solution)/shard_map/all_gather | solution.py:75
  371.9 8.5 fusion.25
  380.3 0.0 reduce-scatter.8.cloned.1.call-update
  380.4 0.0 reduce-scatter.10.cloned.1.call-start
  380.4 0.1 convert_reduce_fusion
  380.6 21.4 %reduce-scatter.8.cloned.1.call-done = f32[32,1536]{1,0:T(8,128)} async-done(((f32[128,1536]{1,0:T(8,128)}), f32[32,1536]{1,0:T(8,128)}) %reduce-scatter.8.cloned.1.call-update) | async-done | bytes 196624 | tf_op jit(solution)/shard_map/reduce_scatter | solution.py:86
  402.0 1.1 multiply_reduce_fusion
  403.0 0.1 convolution_bitcast_fusion.2
  403.1 39.3 %all-reduce = (f32[16]{0:T(128)S(1)}, f32[16]{0:T(128)S(1)}) all-reduce(f32[16]{0:T(128)S(1)} %convolution_bitcast_fusion.2, f32[16]{0:T(128)S(1)} %broadcast_multiply_fusion.1), channel_id=1, replica_groups=mesh['inp'=2,'hid'=4,'tok'=4] {'inp','hid','tok'}, use_global_device_ids=true, to_apply=%region_3.0 | all-reduce | flops 32 | bytes 256 | tf_op jit(solution)/shard_map/psum | solution.py:100
  442.4 0.6 multiply_reduce_fusion.1
  443.1 0.1 convolution_bitcast_fusion.1
  443.2 0.1 broadcast_multiply_fusion
  443.3 9.4 all_gather.28
  452.7 13.0 %fusion.26 = f32[128,1536]{1,0:T(8,128)} fusion(f32[128,1536]{1,0:T(8,128)S(1)} %all_gather.28, f32[1536,1536]{1,0:T(8,128)} %all-gather.7.cloned.1.call-done), kind=kOutput, calls=%fused_computation.47 | convolution fusion | flops 3623878656 | bytes 11010048 | tf_op jit(solution)/shard_map/dot_general | solution.py:108
  465.7 0.2 reduce-scatter.14.cloned.1.call-start
  466.0 10.0 fusion.27
  476.0 0.0 reduce-scatter.14.cloned.1.call-update
  476.0 0.0 reduce-scatter.12.cloned.1.call-start
  476.0 6.4 reduce-scatter.10.cloned.1.call-done
  482.4 1.2 fusion.7
  483.7 11.5 all_gather.29
  495.2 10.1 convolution_bitcast_fusion
  505.3 0.3 all-gather.11.cloned.1.call-start
  505.6 1.4 copy-done
  507.0 1.9 copy.49
  508.9 3.2 copy.46
  512.1 1.9 copy.48
  514.0 3.2 copy.52
  517.2 129.4 %reduce-scatter.14.cloned.1.call-done = f32[384,1536]{0,1:T(8,128)} async-done(((f32[1536,1536]{0,1:T(8,128)}), f32[384,1536]{0,1:T(8,128)}) %reduce-scatter.14.cloned.1.call-update) | async-done | bytes 2359312 | tf_op jit(solution)/shard_map/reduce_scatter | solution.py:105
  646.6 8.7 multiply_add_fusion
  655.4 0.0 all-gather.11.cloned.1.call-update
  655.4 0.0 all-gather.9.cloned.1.call-start
  655.4 2.2 copy-done.1
  657.6 1.9 copy.44
  659.6 3.2 copy.42
  662.8 1.9 copy.43
  664.7 3.2 copy.51
  667.9 143.9 %reduce-scatter.12.cloned.1.call-done = f32[384,1536]{0,1:T(8,128)} async-done(((f32[1536,1536]{0,1:T(8,128)}), f32[384,1536]{0,1:T(8,128)}) %reduce-scatter.12.cloned.1.call-update) | async-done | bytes 2359312 | tf_op jit(solution)/shard_map/reduce_scatter | solution.py:112
  811.8 8.7 multiply_add_fusion.1
  821.4 1.2 copy-done.3
  822.6 1.9 copy.60
  824.5 3.3 copy.56
  827.8 1.9 copy.58
  829.8 3.0 copy.59
  832.8 3.2 copy.55
  836.0 1.9 copy.57
  838.0 143.2 %all-gather.11.cloned.1.call-done = f32[1536,1536]{0,1:T(8,128)} async-done(((f32[384,1536]{0,1:T(8,128)}), f32[1536,1536]{0,1:T(8,128)}) %all-gather.11.cloned.1.call-update) | async-done | bytes 9437200 | tf_op jit(solution)/shard_map/all_gather | solution.py:119
  981.1 9.8 copy.54
  990.9 157.4 %all-gather.9.cloned.1.call-done = f32[1536,1536]{0,1:T(8,128)} async-done(((f32[384,1536]{0,1:T(8,128)}), f32[1536,1536]{0,1:T(8,128)}) %all-gather.9.cloned.1.call-update) | async-done | bytes 9437200 | tf_op jit(solution)/shard_map/all_gather | solution.py:118
  1148.3 9.6 copy.53
  (32 shorter events, 0.1 us)
Async XLA Ops:
  7.2 0.9 copy-start.11
  7.2 171.9 %all-gather.5.cloned.1.call-start = ((), (), s32[]{:S(2)}) async-start(), calls=%async_computation.5 | async-start | bytes 11796480 | tf_op jit(solution)/shard_map/all_gather | solution.py:78
  7.9 195.5 %reduce-scatter.6.cloned.1.call-start = ((), (), s32[]{:S(2)}) async-start(), calls=%async_computation.6 | async-start | bytes 1179648 | tf_op jit(solution)/shard_map/reduce_scatter | solution.py:82
  187.6 184.3 %all-gather.7.cloned.1.call-start = ((), (), s32[]{:S(2)}) async-start(), calls=%async_computation.7 | async-start | bytes 11796480 | tf_op jit(solution)/shard_map/all_gather | solution.py:75
  188.3 213.6 %reduce-scatter.8.cloned.1.call-start = ((), (), s32[]{:S(2)}) async-start(), calls=%async_computation.8 | async-start | bytes 983040 | tf_op jit(solution)/shard_map/reduce_scatter | solution.py:86
  216.0 164.4 %copy-start.15 = (s32[32]{0:T(128)S(1)}, s32[32]{0:T(128)}, u32[]{:S(2)}) copy-start(s32[32]{0:T(128)} %param.16) | copy-start | bytes 388
  216.0 185.9 %copy-start.10 = (f32[32,1536]{1,0:T(8,128)S(1)}, f32[32,1536]{1,0:T(8,128)}, u32[]{:S(2)}) copy-start(f32[32,1536]{1,0:T(8,128)} %param.15) | copy-start | bytes 589828
  216.0 226.4 %copy-start.12 = (f32[16]{0:T(128)S(1)}, f32[16]{0:T(128)}, u32[]{:S(2)}) copy-start(f32[16]{0:T(128)} %param.19) | copy-start | bytes 196
  216.0 226.4 %copy-start.13 = (f32[16]{0:T(128)S(1)}, f32[16]{0:T(128)}, u32[]{:S(2)}) copy-start(f32[16]{0:T(128)} %param.18) | copy-start | bytes 196
  216.1 226.4 %copy-start.14 = (s32[16]{0:T(128)S(1)}, s32[16]{0:T(128)}, u32[]{:S(2)}) copy-start(s32[16]{0:T(128)} %param.17) | copy-start | bytes 196
  380.4 102.0 %reduce-scatter.10.cloned.1.call-start = ((), (), s32[]{:S(2)}) async-start(), calls=%async_computation.9 | async-start | bytes 1179648 | tf_op jit(solution)/shard_map/reduce_scatter | solution.py:109
  465.7 180.9 %reduce-scatter.14.cloned.1.call-start = ((), (), s32[]{:S(2)}) async-start(), calls=%async_computation.12 | async-start | bytes 11796480 | tf_op jit(solution)/shard_map/reduce_scatter | solution.py:105
  476.0 6.5 copy-start.9
  476.0 335.8 %reduce-scatter.12.cloned.1.call-start = ((), (), s32[]{:S(2)}) async-start(), calls=%async_computation.10 | async-start | bytes 11796480 | tf_op jit(solution)/shard_map/reduce_scatter | solution.py:112
  505.3 1.7 copy-start
  505.3 475.8 %all-gather.11.cloned.1.call-start = ((), (), s32[]{:S(2)}) async-start(), calls=%async_computation.13 | async-start | bytes 11796480 | tf_op jit(solution)/shard_map/all_gather | solution.py:119
  508.9 3.2 copy-start.7
  514.0 132.6 %copy-start.5 = (f32[384,1536]{0,1:T(8,128)S(1)}, f32[384,1536]{0,1:T(8,128)}, u32[]{:S(2)}) copy-start(f32[384,1536]{0,1:T(8,128)} %copy.49) | copy-start | bytes 7077892
  655.4 2.3 copy-start.1
  655.4 492.9 %all-gather.9.cloned.1.call-start = ((), (), s32[]{:S(2)}) async-start(), calls=%async_computation.11 | async-start | bytes 11796480 | tf_op jit(solution)/shard_map/all_gather | solution.py:118
  659.6 3.2 copy-start.8
  664.7 147.1 %copy-start.6 = (f32[384,1536]{0,1:T(8,128)S(1)}, f32[384,1536]{0,1:T(8,128)}, u32[]{:S(2)}) copy-start(f32[384,1536]{0,1:T(8,128)} %copy.44) | copy-start | bytes 7077892
  820.6 2.0 copy-start.3
  824.5 3.3 copy-start.2
  832.8 3.2 copy-start.4
Sparse Core Ops, SparseCore 0:
  9.6 169.4 all-gather.4
  187.7 15.6 reduce-scatter.5
  205.0 166.7 all-gather.6
  380.5 21.4 reduce-scatter.7
  465.9 16.4 reduce-scatter.9
  485.3 161.2 reduce-scatter.13
  649.7 162.1 reduce-scatter.11
  813.5 167.5 all-gather.10
  983.3 164.9 all-gather.8
where the time goes:
time: 1170 us
  waiting for transfers between devices  935 us (80%)
  blocking collectives  81.8 us (7%)
  local copies, waits for them, and re-layouts  60.2 us (5%)
  matrix products  50.3 us (4%)
  other arithmetic  21.8 us (2%)
  between operations  15.9 us (1%)
    all_gather x1, waiting for transfers between devices, on_device(): lax.all_gather(w_in, 'tok', axis=0, tiled=True)  161 us
    all_gather x1, waiting for transfers between devices, on_device(): lax.all_gather(weight_in, 'tok', axis=0, tiled=True)  157 us
    all_gather x1, waiting for transfers between devices, on_device(): w_out_block = lax.all_gather(w_out, 'tok', axis=0, tiled=True)  156 us
    reduce_scatter x1, waiting for transfers between devices, on_device(): lax.psum_scatter(contract_rows(picked, d_hidden), 'tok', scatter_dimensio...  144 us
    all_gather x1, waiting for transfers between devices, on_device(): lax.all_gather(weight_out, 'tok', axis=0, tiled=True)  143 us
    reduce_scatter x1, waiting for transfers between devices, on_device(): lax.psum_scatter(contract_rows(picked, d_all), 'tok', scatter_dimension=0...  129 us
    unnamed x48, local copies, waits for them, and re-layouts  60.2 us
    psum x1, blocking collectives, on_device(): sq_sums, counts = lax.psum((local_sq, local_counts), ('inp', 'hid', 'tok'))  39.3 us
  transfers between devices with their start and end apart: 9, of which 9 were waited for; matrix products, arithmetic and copies ran while one was open for 7% of the time, Pallas kernels for 0%

commit v1 on v0

--- a/solution.py
+++ b/solution.py
@@ -8,6 +8,7 @@
 
 
 highest = lax.Precision.HIGHEST
+precise = lax.Precision.HIGH
 gelu_c = 0.7978845608028654
 gelu_k = 0.044715
 kto_beta = 4.0
@@ -52,7 +53,15 @@
 
 
 def contract_rows(left, right):
-    return lax.dot_general(left, right, (((0,), (0,)), ((), ())), precision=highest)
+    return lax.dot_general(left, right, (((0,), (0,)), ((), ())), precision=precise)
+
+
+def gather_rows(block, axis):
+    return lax.all_gather(block, axis, axis=0, tiled=True)
+
+
+def scatter_rows(part, axis):
+    return lax.psum_scatter(part, axis, scatter_dimension=0, tiled=True)
 
 
 def on_device(
@@ -71,53 +80,31 @@
     e_in,
     e_out,
 ):
-    all_rows = lax.all_gather(tokens, "hid", axis=0, tiled=True)
-    w_out_block = lax.all_gather(w_out, "tok", axis=0, tiled=True)
-    hidden_part = jnp.dot(
-        all_rows,
-        lax.all_gather(w_in, "tok", axis=0, tiled=True),
-        precision=highest,
-        preferred_element_type=jnp.float32,
+    ids = gather_rows(gather_rows(sample_ids, "tok"), "hid")
+    onehot = (ids[:, None] == jnp.arange(SAMPLES, dtype=jnp.int32)[None, :]).astype(jnp.float32)
+    counts = jnp.sum(onehot, axis=0)
+    columns = lax.all_to_all(tokens, "tok", split_axis=1, concat_axis=0, tiled=True)
+    all_rows = gather_rows(columns, "hid")
+    hidden_part = lax.dot_general(w_in, all_rows, (((0,), (1,)), ((), ())), precision=precise)
+    hidden = lax.psum(scatter_rows(hidden_part, "tok"), "inp")
+    active, slope = gelu_parts(hidden)
+    out_part = contract_rows(active, w_out)
+    output = scatter_rows(scatter_rows(out_part, "hid"), "tok")
+    error = gather_rows(gather_rows(output - targets, "tok"), "hid")
+    token_sq = jnp.sum(error * error, axis=1)
+    sq_sums = lax.psum(jnp.dot(token_sq, onehot, precision=highest), "inp")
+    loss, sample_coef = kto_terms(sq_sums, counts, labels, utility, ref_loss)
+    token_coef = jnp.dot(onehot, sample_coef, precision=highest)
+    grad_out = jnp.dot(active * token_coef[None, :], error, precision=precise)
+    d_active = lax.psum(
+        lax.dot_general(w_out, error, (((1,), (1,)), ((), ())), precision=precise), "inp"
     )
-    hidden_share = lax.psum_scatter(hidden_part, "inp", scatter_dimension=0, tiled=True)
-    active_share, slope_share = gelu_parts(hidden_share)
-    active = lax.all_gather(active_share, "inp", axis=0, tiled=True)
-    picked = active
-    output = lax.psum_scatter(
-        jnp.dot(picked, w_out_block, precision=highest, preferred_element_type=jnp.float32),
-        "hid",
-        scatter_dimension=0,
-        tiled=True,
-    )
-    error_rows = output - targets
-    onehot = (sample_ids[:, None] == jnp.arange(SAMPLES, dtype=jnp.int32)[None, :]).astype(
-        jnp.float32
-    )
-    token_sq = jnp.sum(error_rows * error_rows, axis=1)
-    local_sq = jnp.dot(token_sq, onehot, precision=highest)
-    leading = lax.axis_index("inp") == 0
-    local_counts = jnp.sum(onehot, axis=0) * jnp.where(leading, 1.0, 0.0)
-    sq_sums, counts = lax.psum((local_sq, local_counts), ("inp", "hid", "tok"))
-    loss, sample_coef = kto_terms(sq_sums, counts, labels, utility, ref_loss)
-    d_output = error_rows * jnp.dot(onehot, sample_coef, precision=highest)[:, None]
-    d_all = lax.all_gather(d_output, "hid", axis=0, tiled=True)
-    picked = active
-    grad_out = lax.psum_scatter(
-        contract_rows(picked, d_all), "tok", scatter_dimension=0, tiled=True
-    )
-    d_active = lax.dot_general(d_all, w_out_block, (((1,), (1,)), ((), ())), precision=highest)
-    d_share = lax.psum_scatter(d_active, "inp", scatter_dimension=0, tiled=True) * slope_share
-    d_hidden = lax.all_gather(d_share, "inp", axis=0, tiled=True)
-    picked = all_rows
-    grad_in = lax.psum_scatter(
-        contract_rows(picked, d_hidden), "tok", scatter_dimension=0, tiled=True
-    )
+    d_hidden = gather_rows(d_active * slope * token_coef[None, :], "tok")
+    weight_out, new_m_out, new_v_out, new_e_out = adamw(w_out, m_out, v_out, e_out, grad_out)
+    new_w_out = gather_rows(weight_out, "tok")
+    grad_in = lax.dot_general(all_rows, d_hidden, (((0,), (1,)), ((), ())), precision=precise)
     weight_in, new_m_in, new_v_in, new_e_in = adamw(w_in, m_in, v_in, e_in, grad_in)
-    weight_out, new_m_out, new_v_out, new_e_out = adamw(w_out, m_out, v_out, e_out, grad_out)
-    new_w_in, new_w_out = (
-        lax.all_gather(weight_in, "tok", axis=0, tiled=True),
-        lax.all_gather(weight_out, "tok", axis=0, tiled=True),
-    )
+    new_w_in = gather_rows(weight_in, "tok")
     return (
         loss,
         new_w_in,

time: 1170 us -> 710 us (0.61)
  waiting for transfers between devices: 935 us -> 526 us
  blocking collectives: 81.8 us -> 57.2 us
  other arithmetic: 21.8 us -> 4.74 us
    all_gather x4, waiting for transfers between devices: 617 us -> 339 us  [gather_rows(): return lax.all_gather(block, axis, axis=0, tiled=True)]
    reduce_scatter x5 -> x3, waiting for transfers between devices: 316 us -> 122 us  [scatter_rows(): return lax.psum_scatter(part, axis, scatter_dimension=0, tiled=True)]
    psum x0 -> x2, waiting for transfers between devices: none -> 64.9 us  [the longest x1 36.6 us: on_device(): hidden = lax.psum(scatter_rows(hidden_part, 'tok'), 'inp')]
    psum x1, blocking collectives: 39.3 us -> 4.93 us  [on_device(): sq_sums = lax.psum(jnp.dot(token_sq, onehot, precision=highest), 'inp')]
    add x2 -> x0, other arithmetic: 17.5 us -> none  [adamw(): average = ema_rate * average + (1.0 - ema_rate) * weight]
    all_to_all x0 -> x1, blocking collectives: none -> 13.6 us  [on_device(): lax.all_to_all(tokens, 'tok', split_axis=1, concat_axis=0, tiled=True)]
    all_gather x4 -> x3, blocking collectives: 42.5 us -> 32 us  [gather_rows(): return lax.all_gather(block, axis, axis=0, tiled=True)]
    unnamed x48 -> x51, local copies, waits for them, and re-layouts: 60.2 us -> 61.7 us
  transfers between devices with their start and end apart: 9 -> 9, of which waited for: 9 -> 9; matrix products, arithmetic and copies ran while one was open for 7% -> 10% of each run, Pallas kernels for 0% -> 0%
where the time goes in v1:
time: 710 us; the launch traced here: 709 us
  waiting for transfers between devices  526 us (74%)
  local copies, waits for them, and re-layouts  62.7 us (9%)
  blocking collectives  57.2 us (8%)
  matrix products  41.2 us (6%)
  between operations  16.5 us (2%)
    all_gather x4, waiting for transfers between devices, gather_rows(): return lax.all_gather(block, axis, axis=0, tiled=True)  339 us
    reduce_scatter x3, waiting for transfers between devices, scatter_rows(): return lax.psum_scatter(part, axis, scatter_dimension=0, tiled=True)  122 us
    unnamed x51, local copies, waits for them, and re-layouts  61.7 us
    psum x1, waiting for transfers between devices, on_device(): hidden = lax.psum(scatter_rows(hidden_part, 'tok'), 'inp')  36.6 us
    all_gather x3, blocking collectives, gather_rows(): return lax.all_gather(block, axis, axis=0, tiled=True)  32 us
    psum x1, waiting for transfers between devices, on_device(): lax.psum(lax.dot_general(w_out, error, (((1,), (1,)), ((), ())), precisio...  28.3 us
  transfers between devices with their start and end apart: 9, of which 9 were waited for; matrix products, arithmetic and copies ran while one was open for 10% of the time, Pallas kernels for 0%

profile of v1, /device:TPU:0, one launch (start us, length us, event | category | flops | bytes accessed | tf_op | source)
XLA Modules:
  0.0 709.1 jit_solution(15605983663578961978)
XLA Ops:
  7.2 0.0 reduce-scatter.4.cloned.1.call-start
  7.2 0.9 copy.138
  8.2 13.6 %all_to_all.19 = f32[32,4,384]{2,0,1:T(8,128)S(1)} all-to-all(f32[32,4,384]{2,0,1:T(8,128)S(1)} %bitcast.30), channel_id=1, replica_groups=mesh['inp'=2,'hid'=4,'tok'=4] {'tok'}, dimensions={1} | all-to-all | bytes 393216 | tf_op jit(solution)/shard_map/all_to_all | solution.py:86
  21.8 8.6 %all_gather.24 = f32[512,384]{1,0:T(8,128)S(1)} all-gather(f32[128,384]{1,0:T(8,128)S(1)} %bitcast.31), channel_id=1, replica_groups=mesh['inp'=2,'hid'=4,'tok'=4] {'hid'}, dimensions={0}, use_global_device_ids=true | all-gather | bytes 983040 | tf_op jit(solution)/shard_map/all_gather | solution.py:60
  30.3 0.9 copy-done.7
  31.2 7.2 %fusion.38 = f32[1536,512]{1,0:T(8,128)} fusion(f32[384,1536]{1,0:T(8,128)} %param.20, f32[512,384]{1,0:T(8,128)S(1)} %all_gather.24), kind=kOutput, calls=%fused_computation.57 | convolution fusion | flops 1811939328 | bytes 6291456 | tf_op jit(solution)/shard_map/dot_general | solution.py:88
  38.4 0.0 reduce-scatter.4.cloned.1.call-update
  38.5 0.0 all-reduce.4.cloned.1.call-start
  38.5 58.8 %reduce-scatter.4.cloned.1.call-done = f32[384,512]{1,0:T(8,128)} async-done(((f32[1536,512]{1,0:T(8,128)}), f32[384,512]{1,0:T(8,128)}) %reduce-scatter.4.cloned.1.call-update) | async-done | bytes 786448 | tf_op jit(solution)/shard_map/reduce_scatter | solution.py:64
  97.3 0.0 all-reduce.4.cloned.1.call-update
  97.4 0.0 reduce-scatter.6.cloned.1.call-start
  97.4 36.6 %all-reduce.4.cloned.1.call-done = f32[384,512]{1,0:T(8,128)} async-done(((f32[384,512]{1,0:T(8,128)}), f32[384,512]{1,0:T(8,128)}) %all-reduce.4.cloned.1.call-update) | async-done | bytes 786448 | tf_op jit(solution)/shard_map/psum | solution.py:89
  134.0 5.6 fusion.12
  139.6 0.0 reduce-scatter.8.cloned.1.call-start
  139.7 38.0 %reduce-scatter.6.cloned.1.call-done = f32[128,1536]{1,0:T(8,128)} async-done(((f32[512,1536]{1,0:T(8,128)}), f32[128,1536]{1,0:T(8,128)}) %reduce-scatter.6.cloned.1.call-update) | async-done | bytes 786448 | tf_op jit(solution)/shard_map/reduce_scatter | solution.py:64
  177.7 0.0 reduce-scatter.8.cloned.1.call-update
  177.7 0.0 all-gather.6.cloned.1.call-start
  177.8 25.4 %reduce-scatter.8.cloned.1.call-done = f32[32,1536]{1,0:T(8,128)} async-done(((f32[128,1536]{1,0:T(8,128)}), f32[32,1536]{1,0:T(8,128)}) %reduce-scatter.8.cloned.1.call-update) | async-done | bytes 196624 | tf_op jit(solution)/shard_map/reduce_scatter | solution.py:64
  203.2 0.9 sub.28
  204.2 18.4 %all_gather.25 = f32[128,1536]{1,0:T(8,128)} all-gather(f32[32,1536]{1,0:T(8,128)S(1)} %sub.28), channel_id=1, replica_groups=mesh['inp'=2,'hid'=4,'tok'=4] {'tok'}, dimensions={0}, use_global_device_ids=true | all-gather | bytes 983040 | tf_op jit(solution)/shard_map/all_gather | solution.py:60
  222.6 0.0 all-gather.6.cloned.1.call-update
  222.6 0.0 all-reduce.6.cloned.1.call-start
  222.7 0.6 dynamic-slice
  224.0 0.2 dynamic-update-slice
  224.2 6.7 all-reduce
  230.9 5.0 all-gather
  235.9 0.1 convert_reduce_fusion
  236.0 14.9 %all-gather.6.cloned.1.call-done = f32[512,1536]{1,0:T(8,128)} async-done(((f32[128,1536]{1,0:T(8,128)}), f32[512,1536]{1,0:T(8,128)}) %all-gather.6.cloned.1.call-update) | async-done | bytes 3145744 | tf_op jit(solution)/shard_map/all_gather | solution.py:60
  250.9 5.7 convolution_bitcast_fusion.1
  256.6 0.0 all-reduce.6.cloned.1.call-update
  256.6 0.0 all-gather.8.cloned.1.call-start
  256.7 0.3 multiply_reduce_fusion
  257.0 0.1 convolution_bitcast_fusion.2
  257.1 4.9 psum.22
  262.0 0.6 multiply_reduce_fusion.1
  262.6 0.1 fusion.13
  262.8 28.3 %all-reduce.6.cloned.1.call-done = f32[384,512]{1,0:T(8,128)} async-done(((f32[384,512]{1,0:T(8,128)}), f32[384,512]{1,0:T(8,128)}) %all-reduce.6.cloned.1.call-update) | async-done | bytes 786448 | tf_op jit(solution)/shard_map/psum | solution.py:99
  291.1 2.8 fusion.8
  293.9 0.2 all-gather.12.cloned.1.call-start
  294.1 3.0 copy.122
  297.2 3.0 copy.117
  300.2 3.2 copy.119
  303.4 3.0 copy.125
  306.5 10.0 %multiply_add_fusion = (f32[384,1536]{0,1:T(8,128)}, f32[384,1536]{0,1:T(8,128)}, f32[384,1536]{0,1:T(8,128)}, f32[384,1536]{0,1:T(8,128)}) fusion(f32[384,1536]{0,1:T(8,128)} %copy.125, f32[384,1536]{0,1:T(8,128)} %copy.122, f32[384,1536]{0,1:T(8,128)} %copy.117, f32[384,1536]{0,1:T(8,128)} %copy.119, f32[512,1536]{1,0:T(8,128)S(1)} %copy-done, ...), kind=kOutput, calls=%fused_computation.6 | convolution fusion | flops 1823735808 | bytes 22808576 | tf_op jit(solution)/shard_map/dot_general | solution.py:98
  316.5 0.0 all-gather.12.cloned.1.call-update
  316.5 0.0 all-gather.10.cloned.1.call-start
  316.5 1.6 copy-done.4
  318.1 1.9 copy.115
  320.1 3.2 copy.112
  323.3 1.9 copy.114
  325.2 3.2 copy.124
  328.5 29.1 %all-gather.8.cloned.1.call-done = f32[1536,512]{1,0:T(8,128)} async-done(((f32[384,512]{1,0:T(8,128)}), f32[1536,512]{1,0:T(8,128)}) %all-gather.8.cloned.1.call-update) | async-done | bytes 3145744 | tf_op jit(solution)/shard_map/all_gather | solution.py:60
  357.5 12.4 %multiply_add_fusion.1 = (f32[384,1536]{0,1:T(8,128)}, f32[384,1536]{0,1:T(8,128)}, f32[384,1536]{0,1:T(8,128)}, f32[384,1536]{0,1:T(8,128)}) fusion(f32[384,1536]{0,1:T(8,128)} %copy.124, f32[384,1536]{0,1:T(8,128)S(1)} %copy-done.6, f32[384,1536]{0,1:T(8,128)} %copy.112, f32[384,1536]{0,1:T(8,128)} %copy.114, ...), kind=kOutput, calls=%fused_computation.7 | convolution fusion | flops 1821966336 | bytes 22806528 | tf_op jit(solution)/shard_map/dot_general | solution.py:105
  370.8 1.1 copy-done.3
  371.9 1.9 copy.133
  373.8 3.2 copy.129
  377.0 1.9 copy.131
  379.0 3.1 copy.132
  382.0 3.2 copy.128
  385.2 1.9 copy.130
  387.2 137.5 %all-gather.12.cloned.1.call-done = f32[1536,1536]{0,1:T(8,128)} async-done(((f32[384,1536]{0,1:T(8,128)}), f32[1536,1536]{0,1:T(8,128)}) %all-gather.12.cloned.1.call-update) | async-done | bytes 9437200 | tf_op jit(solution)/shard_map/all_gather | solution.py:60
  524.7 9.8 %copy.127 = f32[1536,1536]{1,0:T(8,128)} copy(f32[1536,1536]{0,1:T(8,128)} %all-gather.12.cloned.1.call-done) | data formatting | bytes 18874368
  534.5 157.4 %all-gather.10.cloned.1.call-done = f32[1536,1536]{0,1:T(8,128)} async-done(((f32[384,1536]{0,1:T(8,128)}), f32[1536,1536]{0,1:T(8,128)}) %all-gather.10.cloned.1.call-update) | async-done | bytes 9437200 | tf_op jit(solution)/shard_map/all_gather | solution.py:60
  691.9 9.6 %copy.126 = f32[1536,1536]{1,0:T(8,128)} copy(f32[1536,1536]{0,1:T(8,128)} %all-gather.10.cloned.1.call-done) | data formatting | bytes 18874368
  (33 shorter events, 0.1 us)
Async XLA Ops:
  7.2 90.2 %reduce-scatter.4.cloned.1.call-start = ((), (), s32[]{:S(2)}) async-start(), calls=%async_computation.4 | async-start | bytes 3932160 | tf_op jit(solution)/shard_map/reduce_scatter | solution.py:64
  30.3 0.9 copy-start.7
  38.4 95.6 %copy-start.1 = (f32[384,1536]{1,0:T(8,128)S(1)}, f32[384,1536]{1,0:T(8,128)}, u32[]{:S(2)}) copy-start(f32[384,1536]{1,0:T(8,128)} %param.21) | copy-start | bytes 7077892
  38.5 95.5 %all-reduce.4.cloned.1.call-start = ((), (), s32[]{:S(2)}) async-start(), calls=%async_computation.5 | async-start | bytes 1572864 | tf_op jit(solution)/shard_map/psum | solution.py:89
  97.4 80.4 %reduce-scatter.6.cloned.1.call-start = ((), (), s32[]{:S(2)}) async-start(), calls=%async_computation.6 | async-start | bytes 3932160 | tf_op jit(solution)/shard_map/reduce_scatter | solution.py:64
  139.6 63.6 %copy-start.10 = (f32[32,1536]{1,0:T(8,128)S(1)}, f32[32,1536]{1,0:T(8,128)}, u32[]{:S(2)}) copy-start(f32[32,1536]{1,0:T(8,128)} %param.15) | copy-start | bytes 589828
  139.6 83.1 %copy-start.15 = (u32[32]{0:T(128)S(1)}, u32[32]{0:T(128)}, u32[]{:S(2)}) copy-start(u32[32]{0:T(128)} %constant.59) | copy-start | bytes 388
  139.6 84.3 %copy-start.14 = (s32[32]{0:T(128)S(1)}, s32[32]{0:T(128)}, u32[]{:S(2)}) copy-start(s32[32]{0:T(128)} %param.16) | copy-start | bytes 388
  139.6 63.6 %reduce-scatter.8.cloned.1.call-start = ((), (), s32[]{:S(2)}) async-start(), calls=%async_computation.7 | async-start | bytes 983040 | tf_op jit(solution)/shard_map/reduce_scatter | solution.py:64
  177.7 73.2 %all-gather.6.cloned.1.call-start = ((), (), s32[]{:S(2)}) async-start(), calls=%async_computation.8 | async-start | bytes 3932160 | tf_op jit(solution)/shard_map/all_gather | solution.py:60
  222.6 68.5 %all-reduce.6.cloned.1.call-start = ((), (), s32[]{:S(2)}) async-start(), calls=%async_computation.9 | async-start | bytes 1572864 | tf_op jit(solution)/shard_map/psum | solution.py:99
  250.9 5.8 copy-start
  256.6 5.4 copy-start.11
  256.6 5.4 copy-start.12
  256.6 5.4 copy-start.13
  256.6 100.9 %all-gather.8.cloned.1.call-start = ((), (), s32[]{:S(2)}) async-start(), calls=%async_computation.10 | async-start | bytes 3932160 | tf_op jit(solution)/shard_map/all_gather | solution.py:60
  293.9 230.8 %all-gather.12.cloned.1.call-start = ((), (), s32[]{:S(2)}) async-start(), calls=%async_computation.12 | async-start | bytes 11796480 | tf_op jit(solution)/shard_map/all_gather | solution.py:60
  316.5 1.7 copy-start.4
  316.5 375.4 %all-gather.10.cloned.1.call-start = ((), (), s32[]{:S(2)}) async-start(), calls=%async_computation.11 | async-start | bytes 11796480 | tf_op jit(solution)/shard_map/all_gather | solution.py:60
  320.1 3.2 copy-start.9
  325.2 32.3 %copy-start.6 = (f32[384,1536]{0,1:T(8,128)S(1)}, f32[384,1536]{0,1:T(8,128)}, u32[]{:S(2)}) copy-start(f32[384,1536]{0,1:T(8,128)} %copy.115) | copy-start | bytes 7077892
  325.2 32.3 %copy-start.8 = (f32[512,384]{1,0:T(8,128)S(1)}, f32[512,384]{1,0:T(8,128)}, u32[]{:S(2)}) copy-start(f32[512,384]{1,0:T(8,128)} %copy-done.7) | copy-start | bytes 2359300
  370.0 1.9 copy-start.3
  373.8 3.2 copy-start.2
  382.0 3.2 copy-start.5
Sparse Core Ops, SparseCore 0:
  38.6 58.7 reduce-scatter.3
  99.6 34.3 all-reduce.3
  139.7 37.9 reduce-scatter.5
  179.9 23.3 reduce-scatter.7
  222.8 28.1 all-gather.5
  256.7 34.3 all-reduce.5
  294.0 63.4 all-gather.7
  359.2 165.4 all-gather.11
  526.9 164.9 all-gather.9

commit v2 on v1

--- a/solution.py
+++ b/solution.py
@@ -64,6 +64,21 @@
     return lax.psum_scatter(part, axis, scatter_dimension=0, tiled=True)
 
 
+def spread_rows(block, axis):
+    size = lax.axis_size(axis)
+    before, after = [], []
+    rightward = leftward = block
+    for step in range(size - 1):
+        rightward = lax.ppermute(rightward, axis, [(i, i + 1) for i in range(step, size - 1)])
+        leftward = lax.ppermute(leftward, axis, [(i + 1, i) for i in range(size - 1 - step)])
+        before.insert(0, rightward)
+        after.append(leftward)
+    line = jnp.concatenate(before + [block] + after, axis=0)
+    rows = block.shape[0]
+    start = (size - 1 - lax.axis_index(axis)) * rows
+    return lax.dynamic_slice_in_dim(line, start, size * rows, axis=0)
+
+
 def on_device(
     tokens,
     targets,
@@ -101,10 +116,10 @@
     )
     d_hidden = gather_rows(d_active * slope * token_coef[None, :], "tok")
     weight_out, new_m_out, new_v_out, new_e_out = adamw(w_out, m_out, v_out, e_out, grad_out)
-    new_w_out = gather_rows(weight_out, "tok")
+    new_w_out = spread_rows(weight_out, "tok")
     grad_in = lax.dot_general(all_rows, d_hidden, (((0,), (1,)), ((), ())), precision=precise)
     weight_in, new_m_in, new_v_in, new_e_in = adamw(w_in, m_in, v_in, e_in, grad_in)
-    new_w_in = gather_rows(weight_in, "tok")
+    new_w_in = spread_rows(weight_in, "tok")
     return (
         loss,
         new_w_in,

time: 710 us -> 705 us (level)
  waiting for transfers between devices: 526 us -> 497 us
  starting transfers between devices: 0.55 us -> 28.6 us
    all_gather x4 -> x2, waiting for transfers between devices: 339 us -> 14.9 us  [gather_rows(): return lax.all_gather(block, axis, axis=0, tiled=True)]
    ppermute x0 -> x12, waiting for transfers between devices: none -> 295 us  [the longest x6 156 us: spread_rows(): lax.ppermute(leftward, axis, [(i + 1, i) for i in range(size - 1 - step)])]
    ppermute x0 -> x12, starting transfers between devices: none -> 28.4 us  [the longest x6 20.4 us: spread_rows(): lax.ppermute(rightward, axis, [(i, i + 1) for i in range(step, size - 1)])]
    unnamed x51 -> x33, local copies, waits for them, and re-layouts: 61.7 us -> 37.5 us
    dynamic_slice x0 -> x2, local copies, waits for them, and re-layouts: none -> 16.5 us  [spread_rows(): return lax.dynamic_slice_in_dim(line, start, size * rows, axis=0)]
  transfers between devices with their start and end apart: 9 -> 19, of which waited for: 9 -> 13; matrix products, arithmetic and copies ran while one was open for 10% -> 10% of each run, Pallas kernels for 0% -> 0%
where the time goes in v2:
time: 705 us; the launch traced here: 704 us
  waiting for transfers between devices  497 us (70%)
  local copies, waits for them, and re-layouts  59.7 us (8%)
  blocking collectives  57.4 us (8%)
  matrix products  40 us (6%)
  starting transfers between devices  28.6 us (4%)
  between operations  16.7 us (2%)
    ppermute x6, waiting for transfers between devices, spread_rows(): lax.ppermute(leftward, axis, [(i + 1, i) for i in range(size - 1 - step)])  156 us
    ppermute x6, waiting for transfers between devices, spread_rows(): lax.ppermute(rightward, axis, [(i, i + 1) for i in range(step, size - 1)])  139 us
    reduce_scatter x3, waiting for transfers between devices, scatter_rows(): return lax.psum_scatter(part, axis, scatter_dimension=0, tiled=True)  122 us
    unnamed x33, local copies, waits for them, and re-layouts  37.5 us
    psum x1, waiting for transfers between devices, on_device(): hidden = lax.psum(scatter_rows(hidden_part, 'tok'), 'inp')  36.6 us
    all_gather x3, blocking collectives, gather_rows(): return lax.all_gather(block, axis, axis=0, tiled=True)  32 us
    psum x1, waiting for transfers between devices, on_device(): lax.psum(lax.dot_general(w_out, error, (((1,), (1,)), ((), ())), precisio...  28.1 us
    ppermute x6, starting transfers between devices, spread_rows(): lax.ppermute(rightward, axis, [(i, i + 1) for i in range(step, size - 1)])  20.4 us
  transfers between devices with their start and end apart: 19, of which 13 were waited for; matrix products, arithmetic and copies ran while one was open for 10% of the time, Pallas kernels for 0%

profile of v2, /device:TPU:0, one launch (start us, length us, event | category | flops | bytes accessed | tf_op | source)
XLA Modules:
  0.0 704.2 jit_solution(4686983465539170713)
XLA Ops:
  7.2 0.9 copy.32
  8.2 13.6 %all_to_all.19 = f32[32,4,384]{2,0,1:T(8,128)S(1)} all-to-all(f32[32,4,384]{2,0,1:T(8,128)S(1)} %bitcast.30), channel_id=1, replica_groups=mesh['inp'=2,'hid'=4,'tok'=4] {'tok'}, dimensions={1} | all-to-all | bytes 393216 | tf_op jit(solution)/shard_map/all_to_all | solution.py:101
  21.8 8.6 %all_gather.18 = f32[512,384]{1,0:T(8,128)S(1)} all-gather(f32[128,384]{1,0:T(8,128)S(1)} %bitcast.31), channel_id=1, replica_groups=mesh['inp'=2,'hid'=4,'tok'=4] {'hid'}, dimensions={0}, use_global_device_ids=true | all-gather | bytes 983040 | tf_op jit(solution)/shard_map/all_gather | solution.py:60
  30.3 0.9 copy-done.2
  31.2 7.2 %fusion.38 = f32[1536,512]{1,0:T(8,128)} fusion(f32[384,1536]{1,0:T(8,128)} %param.20, f32[512,384]{1,0:T(8,128)S(1)} %all_gather.18), kind=kOutput, calls=%fused_computation.73 | convolution fusion | flops 1811939328 | bytes 6291456 | tf_op jit(solution)/shard_map/dot_general | solution.py:103
  38.5 58.8 %reduce-scatter.4.cloned.1.call-done = f32[384,512]{1,0:T(8,128)} async-done(((f32[1536,512]{1,0:T(8,128)}), f32[384,512]{1,0:T(8,128)}) %reduce-scatter.4.cloned.1.call-update) | async-done | bytes 786448 | tf_op jit(solution)/shard_map/reduce_scatter | solution.py:64
  97.4 36.6 %all-reduce.4.cloned.1.call-done = f32[384,512]{1,0:T(8,128)} async-done(((f32[384,512]{1,0:T(8,128)}), f32[384,512]{1,0:T(8,128)}) %all-reduce.4.cloned.1.call-update) | async-done | bytes 786448 | tf_op jit(solution)/shard_map/psum | solution.py:104
  134.0 5.6 fusion.12
  139.7 38.0 %reduce-scatter.6.cloned.1.call-done = f32[128,1536]{1,0:T(8,128)} async-done(((f32[512,1536]{1,0:T(8,128)}), f32[128,1536]{1,0:T(8,128)}) %reduce-scatter.6.cloned.1.call-update) | async-done | bytes 786448 | tf_op jit(solution)/shard_map/reduce_scatter | solution.py:64
  177.8 25.4 %reduce-scatter.8.cloned.1.call-done = f32[32,1536]{1,0:T(8,128)} async-done(((f32[128,1536]{1,0:T(8,128)}), f32[32,1536]{1,0:T(8,128)}) %reduce-scatter.8.cloned.1.call-update) | async-done | bytes 196624 | tf_op jit(solution)/shard_map/reduce_scatter | solution.py:64
  203.2 0.9 sub.32
  204.2 18.4 %all_gather.19 = f32[128,1536]{1,0:T(8,128)} all-gather(f32[32,1536]{1,0:T(8,128)S(1)} %sub.32), channel_id=1, replica_groups=mesh['inp'=2,'hid'=4,'tok'=4] {'tok'}, dimensions={0}, use_global_device_ids=true | all-gather | bytes 983040 | tf_op jit(solution)/shard_map/all_gather | solution.py:60
  222.6 0.0 all-reduce.6.cloned.1.call-start
  222.7 0.6 dynamic-slice
  224.0 0.2 dynamic-update-slice
  224.2 6.7 all-reduce
  230.9 5.0 all-gather
  235.9 0.1 convert_reduce_fusion
  236.0 14.9 %all-gather.4.cloned.1.call-done = f32[512,1536]{1,0:T(8,128)} async-done(((f32[128,1536]{1,0:T(8,128)}), f32[512,1536]{1,0:T(8,128)}) %all-gather.4.cloned.1.call-update) | async-done | bytes 3145744 | tf_op jit(solution)/shard_map/all_gather | solution.py:60
  250.9 5.7 convolution_bitcast_fusion.1
  256.7 0.3 multiply_reduce_fusion
  257.0 0.1 convolution_bitcast_fusion.2
  257.1 5.1 psum.22
  262.2 0.6 multiply_reduce_fusion.1
  262.8 0.1 fusion.13
  263.0 28.1 %all-reduce.6.cloned.1.call-done = f32[384,512]{1,0:T(8,128)} async-done(((f32[384,512]{1,0:T(8,128)}), f32[384,512]{1,0:T(8,128)}) %all-reduce.6.cloned.1.call-update) | async-done | bytes 786448 | tf_op jit(solution)/shard_map/psum | solution.py:114
  291.1 2.8 fusion.8
  293.9 9.6 %multiply_add_fusion = (f32[384,1536]{1,0:T(8,128)}, f32[384,1536]{1,0:T(8,128)}, f32[384,1536]{1,0:T(8,128)}, f32[384,1536]{1,0:T(8,128)}) fusion(f32[384,1536]{1,0:T(8,128)} %param.27, f32[384,1536]{1,0:T(8,128)} %param.21, f32[384,1536]{1,0:T(8,128)} %param.23, f32[384,1536]{1,0:T(8,128)} %param.25, f32[512,1536]{1,0:T(8,128)S(1)} %copy-done, ...), kind=kOutput, calls=%fused_computation.6 | convolution fusion | flops 1823735808 | bytes 22808576 | tf_op jit(solution)/shard_map/dot_general | solution.py:113
  303.4 4.8 collective-permute-start.6
  308.2 1.3 collective-permute-start.9
  309.5 94.3 %collective-permute-done.6 = f32[384,1536]{1,0:T(8,128)} collective-permute-done((f32[384,1536]{1,0:T(8,128)}, f32[384,1536]{1,0:T(8,128)}, u32[]{:S(2)}, u32[]{:S(2)}) %collective-permute-start.6) | collective-permute-done | bytes 2359328 | tf_op jit(solution)/shard_map/ppermute | solution.py:72
  403.8 2.1 collective-permute-start.7
  405.9 11.7 %multiply_add_fusion.1 = (f32[384,1536]{1,0:T(8,128)}, f32[384,1536]{1,0:T(8,128)S(1)}, f32[384,1536]{1,0:T(8,128)}, f32[384,1536]{1,0:T(8,128)}) fusion(f32[384,1536]{1,0:T(8,128)} %param.26, f32[384,1536]{1,0:T(8,128)} %param.20, f32[384,1536]{1,0:T(8,128)} %param.22, f32[384,1536]{1,0:T(8,128)} %param.24, f32[1536,512]{1,0:T(8,128)} %all-gather.6.cloned.1.call-done, ...), kind=kOutput, calls=%fused_computation.7 | convolution fusion | flops 1821966336 | bytes 22806528 | tf_op jit(solution)/shard_map/dot_general | solution.py:120
  417.6 8.6 %collective-permute-start = (f32[384,1536]{1,0:T(8,128)S(1)}, f32[384,1536]{1,0:T(8,128)}, u32[]{:S(2)}, u32[]{:S(2)}) collective-permute-start(f32[384,1536]{1,0:T(8,128)S(1)} %get-tuple-element.14), channel_id=1, source_target_pairs={{0,1},{1,2},{2,3},{4,5},{5,6},{6,7},{8,9},{9,10},{10,11},{12,13},{... | collective-permute-start | bytes 7077896 | tf_op jit(solution)/shard_map/ppermute | solution.py:72
  426.2 1.3 collective-permute-start.10
  427.5 1.3 collective-permute-start.3
  428.8 2.0 collective-permute-start.8
  430.8 44.3 %collective-permute-done = f32[384,1536]{1,0:T(8,128)} collective-permute-done((f32[384,1536]{1,0:T(8,128)S(1)}, f32[384,1536]{1,0:T(8,128)}, u32[]{:S(2)}, u32[]{:S(2)}) %collective-permute-start) | collective-permute-done | bytes 2359328 | tf_op jit(solution)/shard_map/ppermute | solution.py:72
  475.1 2.1 collective-permute-start.1
  477.2 5.3 collective-permute-done.10
  482.6 1.3 collective-permute-start.11
  483.9 49.3 %collective-permute-done.3 = f32[384,1536]{1,0:T(8,128)} collective-permute-done((f32[384,1536]{1,0:T(8,128)S(1)}, f32[384,1536]{1,0:T(8,128)}, u32[]{:S(2)}, u32[]{:S(2)}) %collective-permute-start.3) | collective-permute-done | bytes 2359328 | tf_op jit(solution)/shard_map/ppermute | solution.py:73
  533.1 1.3 collective-permute-start.4
  535.1 3.2 constant_dynamic-update-slice_fusion.13
  538.3 3.2 constant_dynamic-update-slice_fusion.12
  541.6 0.8 collective-permute-start.2
  542.4 3.3 constant_dynamic-update-slice_fusion.11
  545.6 3.3 constant_dynamic-update-slice_fusion.10
  548.9 3.2 constant_dynamic-update-slice_fusion.9
  552.1 3.3 constant_dynamic-update-slice_fusion.8
  555.4 28.3 %collective-permute-done.11 = f32[384,1536]{1,0:T(8,128)} collective-permute-done((f32[384,1536]{1,0:T(8,128)}, f32[384,1536]{1,0:T(8,128)}, u32[]{:S(2)}, u32[]{:S(2)}) %collective-permute-start.11) | collective-permute-done | bytes 2359328 | tf_op jit(solution)/shard_map/ppermute | solution.py:73
  583.7 3.2 constant_dynamic-update-slice_fusion.7
  586.9 45.7 %collective-permute-done.4 = f32[384,1536]{1,0:T(8,128)} collective-permute-done((f32[384,1536]{1,0:T(8,128)}, f32[384,1536]{1,0:T(8,128)}, u32[]{:S(2)}, u32[]{:S(2)}) %collective-permute-start.4) | collective-permute-done | bytes 2359328 | tf_op jit(solution)/shard_map/ppermute | solution.py:73
  632.7 1.5 collective-permute-start.5
  634.2 8.3 %constant_dynamic-slice_fusion = f32[1536,1536]{1,0:T(8,128)} fusion(f32[2688,1536]{1,0:T(8,128)} %constant_dynamic-update-slice_fusion.7, s32[]{:T(128)S(6)} %select_n.4), kind=kLoop, calls=%fused_computation.48 | loop fusion | bytes 18874372 | tf_op jit(solution)/shard_map/dynamic_slice | solution.py:79
  642.5 1.6 constant_dynamic-update-slice_fusion.6
  644.0 3.2 constant_dynamic-update-slice_fusion.5
  647.3 3.3 constant_dynamic-update-slice_fusion.4
  650.5 1.6 constant_dynamic-update-slice_fusion.3
  652.2 3.2 constant_dynamic-update-slice_fusion.2
  655.4 3.3 constant_dynamic-update-slice_fusion.1
  658.7 27.8 %collective-permute-done.5 = f32[384,1536]{1,0:T(8,128)S(1)} collective-permute-done((f32[384,1536]{1,0:T(8,128)}, f32[384,1536]{1,0:T(8,128)S(1)}, u32[]{:S(2)}, u32[]{:S(2)}) %collective-permute-start.5) | collective-permute-done | bytes 2359328 | tf_op jit(solution)/shard_map/ppermute | solution.py:73
  686.4 1.6 constant_dynamic-update-slice_fusion
  688.0 8.3 %constant_dynamic-slice_fusion.1 = f32[1536,1536]{1,0:T(8,128)} fusion(f32[2688,1536]{1,0:T(8,128)} %constant_dynamic-update-slice_fusion, s32[]{:T(128)S(6)} %select_n.4), kind=kLoop, calls=%fused_computation.49 | loop fusion | bytes 18874372 | tf_op jit(solution)/shard_map/dynamic_slice | solution.py:79
  (37 shorter events, 0.4 us)
Async XLA Ops:
  7.2 90.2 %reduce-scatter.4.cloned.1.call-start = ((), (), s32[]{:S(2)}) async-start(), calls=%async_computation.4 | async-start | bytes 3932160 | tf_op jit(solution)/shard_map/reduce_scatter | solution.py:64
  30.3 0.9 copy-start.2
  38.4 95.6 %copy-start.1 = (f32[384,1536]{1,0:T(8,128)S(1)}, f32[384,1536]{1,0:T(8,128)}, u32[]{:S(2)}) copy-start(f32[384,1536]{1,0:T(8,128)} %param.21) | copy-start | bytes 7077892
  38.5 95.5 %all-reduce.4.cloned.1.call-start = ((), (), s32[]{:S(2)}) async-start(), calls=%async_computation.5 | async-start | bytes 1572864 | tf_op jit(solution)/shard_map/psum | solution.py:104
  97.4 80.4 %reduce-scatter.6.cloned.1.call-start = ((), (), s32[]{:S(2)}) async-start(), calls=%async_computation.6 | async-start | bytes 3932160 | tf_op jit(solution)/shard_map/reduce_scatter | solution.py:64
  139.6 63.6 %copy-start.3 = (f32[32,1536]{1,0:T(8,128)S(1)}, f32[32,1536]{1,0:T(8,128)}, u32[]{:S(2)}) copy-start(f32[32,1536]{1,0:T(8,128)} %param.15) | copy-start | bytes 589828
  139.6 83.1 %copy-start.8 = (u32[32]{0:T(128)S(1)}, u32[32]{0:T(128)}, u32[]{:S(2)}) copy-start(u32[32]{0:T(128)} %constant.71) | copy-start | bytes 388
  139.6 84.3 %copy-start.7 = (s32[32]{0:T(128)S(1)}, s32[32]{0:T(128)}, u32[]{:S(2)}) copy-start(s32[32]{0:T(128)} %param.16) | copy-start | bytes 388
  139.6 63.6 %reduce-scatter.8.cloned.1.call-start = ((), (), s32[]{:S(2)}) async-start(), calls=%async_computation.7 | async-start | bytes 983040 | tf_op jit(solution)/shard_map/reduce_scatter | solution.py:64
  177.7 73.2 %all-gather.4.cloned.1.call-start = ((), (), s32[]{:S(2)}) async-start(), calls=%async_computation.8 | async-start | bytes 3932160 | tf_op jit(solution)/shard_map/all_gather | solution.py:60
  222.6 68.5 %all-reduce.6.cloned.1.call-start = ((), (), s32[]{:S(2)}) async-start(), calls=%async_computation.9 | async-start | bytes 1572864 | tf_op jit(solution)/shard_map/psum | solution.py:114
  250.9 5.8 copy-start
  256.6 5.6 copy-start.4
  256.6 5.6 copy-start.5
  256.6 5.6 copy-start.6
  256.6 149.3 %all-gather.6.cloned.1.call-start = ((), (), s32[]{:S(2)}) async-start(), calls=%async_computation.10 | async-start | bytes 3932160 | tf_op jit(solution)/shard_map/all_gather | solution.py:60
  303.4 100.3 %collective-permute-start.6 = (f32[384,1536]{1,0:T(8,128)}, f32[384,1536]{1,0:T(8,128)}, u32[]{:S(2)}, u32[]{:S(2)}) collective-permute-start(f32[384,1536]{1,0:T(8,128)} %get-tuple-element.10), channel_id=1, source_target_pairs={{0,1},{1,2},{2,3},{4,5},{5,6},{6,7},{8,9},{9,10},{10,11},{12,13},{... | collective-permute-start | bytes 7077896 | tf_op jit(solution)/shard_map/ppermute | solution.py:72
  308.2 118.0 %collective-permute-start.9 = (f32[384,1536]{1,0:T(8,128)}, f32[384,1536]{1,0:T(8,128)}, u32[]{:S(2)}, u32[]{:S(2)}) collective-permute-start(f32[384,1536]{1,0:T(8,128)} %get-tuple-element.10), channel_id=1, source_target_pairs={{1,0},{2,1},{3,2},{5,4},{6,5},{7,6},{9,8},{10,9},{11,10},{13,12},{... | collective-permute-start | bytes 7077896 | tf_op jit(solution)/shard_map/ppermute | solution.py:73
  403.8 25.0 %collective-permute-start.7 = (f32[384,1536]{1,0:T(8,128)}, f32[384,1536]{1,0:T(8,128)}, u32[]{:S(2)}, u32[]{:S(2)}) collective-permute-start(f32[384,1536]{1,0:T(8,128)} %collective-permute-done.6), channel_id=1, source_target_pairs={{1,2},{2,3},{5,6},{6,7},{9,10},{10,11},{13,14},{14,15},{17,18},{18... | collective-permute-start | bytes 7077896 | tf_op jit(solution)/shard_map/ppermute | solution.py:72
  417.6 57.5 %collective-permute-start = (f32[384,1536]{1,0:T(8,128)S(1)}, f32[384,1536]{1,0:T(8,128)}, u32[]{:S(2)}, u32[]{:S(2)}) collective-permute-start(f32[384,1536]{1,0:T(8,128)S(1)} %get-tuple-element.14), channel_id=1, source_target_pairs={{0,1},{1,2},{2,3},{4,5},{5,6},{6,7},{8,9},{9,10},{10,11},{12,13},{... | collective-permute-start | bytes 7077896 | tf_op jit(solution)/shard_map/ppermute | solution.py:72
  426.2 56.4 %collective-permute-start.10 = (f32[384,1536]{1,0:T(8,128)}, f32[384,1536]{1,0:T(8,128)}, u32[]{:S(2)}, u32[]{:S(2)}) collective-permute-start(f32[384,1536]{1,0:T(8,128)} %collective-permute-done.9), channel_id=1, source_target_pairs={{1,0},{2,1},{5,4},{6,5},{9,8},{10,9},{13,12},{14,13},{17,16},{18,1... | collective-permute-start | bytes 7077896 | tf_op jit(solution)/shard_map/ppermute | solution.py:73
  427.5 105.7 %collective-permute-start.3 = (f32[384,1536]{1,0:T(8,128)S(1)}, f32[384,1536]{1,0:T(8,128)}, u32[]{:S(2)}, u32[]{:S(2)}) collective-permute-start(f32[384,1536]{1,0:T(8,128)S(1)} %get-tuple-element.14), channel_id=1, source_target_pairs={{1,0},{2,1},{3,2},{5,4},{6,5},{7,6},{9,8},{10,9},{11,10},{13,12},{... | collective-permute-start | bytes 7077896 | tf_op jit(solution)/shard_map/ppermute | solution.py:73
  428.8 106.3 %collective-permute-start.8 = (f32[384,1536]{1,0:T(8,128)}, f32[384,1536]{1,0:T(8,128)}, u32[]{:S(2)}, u32[]{:S(2)}) collective-permute-start(f32[384,1536]{1,0:T(8,128)} %collective-permute-done.7), channel_id=1, source_target_pairs={{2,3},{6,7},{10,11},{14,15},{18,19},{22,23},{26,27},{30,31}} | collective-permute-start | bytes 7077896 | tf_op jit(solution)/shard_map/ppermute | solution.py:72
  475.1 66.4 %collective-permute-start.1 = (f32[384,1536]{1,0:T(8,128)}, f32[384,1536]{1,0:T(8,128)}, u32[]{:S(2)}, u32[]{:S(2)}) collective-permute-start(f32[384,1536]{1,0:T(8,128)} %collective-permute-done), channel_id=1, source_target_pairs={{1,2},{2,3},{5,6},{6,7},{9,10},{10,11},{13,14},{14,15},{17,18},{18... | collective-permute-start | bytes 7077896 | tf_op jit(solution)/shard_map/ppermute | solution.py:72
  482.6 101.1 %collective-permute-start.11 = (f32[384,1536]{1,0:T(8,128)}, f32[384,1536]{1,0:T(8,128)}, u32[]{:S(2)}, u32[]{:S(2)}) collective-permute-start(f32[384,1536]{1,0:T(8,128)} %collective-permute-done.10), channel_id=1, source_target_pairs={{1,0},{5,4},{9,8},{13,12},{17,16},{21,20},{25,24},{29,28}} | collective-permute-start | bytes 7077896 | tf_op jit(solution)/shard_map/ppermute | solution.py:73
  533.1 99.5 %collective-permute-start.4 = (f32[384,1536]{1,0:T(8,128)}, f32[384,1536]{1,0:T(8,128)}, u32[]{:S(2)}, u32[]{:S(2)}) collective-permute-start(f32[384,1536]{1,0:T(8,128)} %collective-permute-done.3), channel_id=1, source_target_pairs={{1,0},{2,1},{5,4},{6,5},{9,8},{10,9},{13,12},{14,13},{17,16},{18,1... | collective-permute-start | bytes 7077896 | tf_op jit(solution)/shard_map/ppermute | solution.py:73
  541.6 100.9 %collective-permute-start.2 = (f32[384,1536]{1,0:T(8,128)}, f32[384,1536]{1,0:T(8,128)S(1)}, u32[]{:S(2)}, u32[]{:S(2)}) collective-permute-start(f32[384,1536]{1,0:T(8,128)} %collective-permute-done.1), channel_id=1, source_target_pairs={{2,3},{6,7},{10,11},{14,15},{18,19},{22,23},{26,27},{30,31}} | collective-permute-start | bytes 7077896 | tf_op jit(solution)/shard_map/ppermute | solution.py:72
  632.7 53.8 %collective-permute-start.5 = (f32[384,1536]{1,0:T(8,128)}, f32[384,1536]{1,0:T(8,128)S(1)}, u32[]{:S(2)}, u32[]{:S(2)}) collective-permute-start(f32[384,1536]{1,0:T(8,128)} %collective-permute-done.4), channel_id=1, source_target_pairs={{1,0},{5,4},{9,8},{13,12},{17,16},{21,20},{25,24},{29,28}} | collective-permute-start | bytes 7077896 | tf_op jit(solution)/shard_map/ppermute | solution.py:73
Sparse Core Ops, SparseCore 0:
  38.6 58.7 reduce-scatter.3
  99.6 34.3 all-reduce.3
  139.7 37.9 reduce-scatter.5
  179.9 23.3 reduce-scatter.7
  222.8 28.1 all-gather.3
  256.7 34.3 all-reduce.5
  294.0 105.0 all-gather.5

commit v3 on v1

--- a/solution.py
+++ b/solution.py
@@ -1,6 +1,10 @@
+import functools
+
 import jax
 import jax.numpy as jnp
 from jax import lax
+from jax.experimental import pallas as pl
+from jax.experimental.pallas import tpu as pltpu
 from jax.sharding import PartitionSpec as P
 
 D = 3072
@@ -62,6 +66,222 @@
 
 def scatter_rows(part, axis):
     return lax.psum_scatter(part, axis, scatter_dimension=0, tiled=True)
+
+
+def split_bf16(value):
+    high = value.astype(jnp.bfloat16)
+    return high, (value - high.astype(jnp.float32)).astype(jnp.bfloat16)
+
+
+def tail_kernel(
+    size,
+    parts,
+    d_part,
+    scale,
+    rows_t,
+    w_in,
+    m_in,
+    v_in,
+    e_in,
+    w_out,
+    all_in,
+    all_out,
+    m_new,
+    v_new,
+    e_new,
+    others,
+    d_all,
+    w_new,
+    rows_high,
+    rows_low,
+    part_send,
+    part_recv,
+    line_send,
+    line_recv,
+    own_sem,
+):
+    me = lax.axis_index("tok")
+    part = lax.axis_index("inp")
+    units, depth = d_part.shape[0], rows_t.shape[0]
+    mesh_ids = pl.DeviceIdType.MESH
+    steps = size - 1
+    has_left, has_right = me > 0, me < size - 1
+
+    barrier = pltpu.get_barrier_semaphore()
+    for hop in range(1, parts):
+        peer = lax.rem(part + hop, parts)
+        pl.semaphore_signal(barrier, inc=1, device_id={"inp": peer}, device_id_type=mesh_ids)
+
+    @pl.when(has_left)
+    def _():
+        pl.semaphore_signal(barrier, inc=1, device_id={"tok": me - 1}, device_id_type=mesh_ids)
+
+    @pl.when(has_right)
+    def _():
+        pl.semaphore_signal(barrier, inc=1, device_id={"tok": me + 1}, device_id_type=mesh_ids)
+
+    beside = has_left.astype(jnp.int32) + has_right.astype(jnp.int32)
+    pl.semaphore_wait(barrier, parts - 1 + beside)
+
+    def part_copy(hop):
+        return pltpu.make_async_remote_copy(
+            src_ref=d_part,
+            dst_ref=others.at[hop - 1],
+            send_sem=part_send.at[hop - 1],
+            recv_sem=part_recv.at[hop - 1],
+            device_id={"inp": lax.rem(part + hop, parts)},
+            device_id_type=mesh_ids,
+        )
+
+    for hop in range(1, parts):
+        part_copy(hop).start()
+
+    def line_copy(kind, way, step, shard, own=None):
+        array, rows = ((d_all, units), (all_out, units), (all_in, depth))[kind]
+        place = array.at[pl.ds(shard * rows, rows)]
+        return pltpu.make_async_remote_copy(
+            src_ref=place if own is None else own,
+            dst_ref=place,
+            send_sem=line_send.at[kind, way, step],
+            recv_sem=line_recv.at[kind, way, step],
+            device_id={"tok": me + (1 if way == 0 else -1)},
+            device_id_type=mesh_ids,
+        )
+
+    def send_own(kind, own):
+        @pl.when(has_right)
+        def _():
+            line_copy(kind, 0, 0, me, own).start()
+
+        @pl.when(has_left)
+        def _():
+            line_copy(kind, 1, 0, me, own).start()
+
+    def pass_on(kind, step):
+        @pl.when(me - 1 - step >= 0)
+        def _():
+            line_copy(kind, 0, step, me - 1 - step).wait_recv()
+            if step + 1 < steps:
+
+                @pl.when(has_right)
+                def _():
+                    line_copy(kind, 0, step + 1, me - 1 - step).start()
+
+        @pl.when(me + 1 + step < size)
+        def _():
+            line_copy(kind, 1, step, me + 1 + step).wait_recv()
+            if step + 1 < steps:
+
+                @pl.when(has_left)
+                def _():
+                    line_copy(kind, 1, step + 1, me + 1 + step).start()
+
+    def end_sends(kind):
+        for step in range(steps):
+
+            @pl.when((me - step >= 0) & has_right)
+            def _():
+                line_copy(kind, 0, step, me - step).wait_send()
+
+            @pl.when((me + step < size) & has_left)
+            def _():
+                line_copy(kind, 1, step, me + step).wait_send()
+
+    own_out = pltpu.make_async_copy(w_out, all_out.at[pl.ds(me * units, units)], own_sem.at[0])
+    send_own(1, w_out)
+    own_out.start()
+    high, low = split_bf16(rows_t[...])
+    rows_high[...] = high
+    rows_low[...] = low
+
+    for hop in range(1, parts):
+        part_copy(hop).wait_recv()
+    mine = pl.ds(me * units, units)
+    total = d_part[...]
+    for hop in range(1, parts):
+        total = total + others[hop - 1]
+    d_all[mine, :] = total * scale[...]
+    send_own(0, d_all.at[mine])
+
+    early = max(steps - 1, 0)
+    for step in range(early):
+        pass_on(0, step)
+    pass_on(1, 0)
+    for step in range(early, steps):
+        pass_on(0, step)
+
+    width = 256
+
+    @pl.loop(0, w_in.shape[1] // width)
+    def _(tile):
+        cols = pl.ds(pl.multiple_of(tile * width, width), width)
+        d_high, d_low = split_bf16(d_all[cols, :])
+
+        def product(left, right):
+            return lax.dot_general(
+                left, right, (((1,), (1,)), ((), ())), preferred_element_type=jnp.float32
+            )
+
+        grad = product(rows_high[...], d_high)
+        grad = grad + (product(rows_low[...], d_high) + product(rows_high[...], d_low))
+        weight, moment_one, moment_two, average = adamw(
+            w_in[:, cols], m_in[:, cols], v_in[:, cols], e_in[:, cols], grad
+        )
+        w_new[:, cols] = weight
+        m_new[:, cols] = moment_one
+        v_new[:, cols] = moment_two
+        e_new[:, cols] = average
+
+    own_in = pltpu.make_async_copy(w_new, all_in.at[pl.ds(me * depth, depth)], own_sem.at[1])
+    send_own(2, w_new)
+    own_in.start()
+    for step in range(steps):
+        if step + 1 < steps:
+            pass_on(1, step + 1)
+        pass_on(2, step)
+    for hop in range(1, parts):
+        part_copy(hop).wait_send()
+    for kind in range(3):
+        end_sends(kind)
+    own_out.wait()
+    own_in.wait()
+
+
+def backward_tail(d_part, scale, rows_t, w_in, m_in, v_in, e_in, w_out):
+    size, parts = lax.axis_size("tok"), lax.axis_size("inp")
+    units, count = d_part.shape
+    depth, wide = w_in.shape
+    hops, steps = max(parts - 1, 1), max(size - 1, 1)
+    in_vmem = pl.BlockSpec(memory_space=pltpu.VMEM)
+    anywhere = pl.BlockSpec(memory_space=pl.ANY)
+    shard = jax.ShapeDtypeStruct((depth, wide), jnp.float32)
+    return pl.pallas_call(
+        functools.partial(tail_kernel, size, parts),
+        out_shape=(
+            jax.ShapeDtypeStruct((size * depth, wide), jnp.float32),
+            jax.ShapeDtypeStruct((size * units, w_out.shape[1]), jnp.float32),
+            shard,
+            shard,
+            shard,
+        ),
+        in_specs=[in_vmem] * 7 + [anywhere],
+        out_specs=(anywhere, anywhere, in_vmem, in_vmem, in_vmem),
+        scratch_shapes=[
+            pltpu.VMEM((hops, units, count), jnp.float32),
+            pltpu.VMEM((size * units, count), jnp.float32),
+            pltpu.VMEM((depth, wide), jnp.float32),
+            pltpu.VMEM((depth, count), jnp.bfloat16),
+            pltpu.VMEM((depth, count), jnp.bfloat16),
+            pltpu.SemaphoreType.DMA((hops,)),
+            pltpu.SemaphoreType.DMA((hops,)),
+            pltpu.SemaphoreType.DMA((3, 2, steps)),
+            pltpu.SemaphoreType.DMA((3, 2, steps)),
+            pltpu.SemaphoreType.DMA((2,)),
+        ],
+        compiler_params=pltpu.CompilerParams(
+            collective_id=0, has_side_effects=True, vmem_limit_bytes=48 * 1024 * 1024
+        ),
+    )(d_part, scale, rows_t, w_in, m_in, v_in, e_in, w_out)
 
 
 def on_device(
@@ -96,15 +316,11 @@
     loss, sample_coef = kto_terms(sq_sums, counts, labels, utility, ref_loss)
     token_coef = jnp.dot(onehot, sample_coef, precision=highest)
     grad_out = jnp.dot(active * token_coef[None, :], error, precision=precise)
-    d_active = lax.psum(
-        lax.dot_general(w_out, error, (((1,), (1,)), ((), ())), precision=precise), "inp"
-    )
-    d_hidden = gather_rows(d_active * slope * token_coef[None, :], "tok")
+    d_part = lax.dot_general(w_out, error, (((1,), (1,)), ((), ())), precision=precise)
     weight_out, new_m_out, new_v_out, new_e_out = adamw(w_out, m_out, v_out, e_out, grad_out)
-    new_w_out = gather_rows(weight_out, "tok")
-    grad_in = lax.dot_general(all_rows, d_hidden, (((0,), (1,)), ((), ())), precision=precise)
-    weight_in, new_m_in, new_v_in, new_e_in = adamw(w_in, m_in, v_in, e_in, grad_in)
-    new_w_in = gather_rows(weight_in, "tok")
+    new_w_in, new_w_out, new_m_in, new_v_in, new_e_in = backward_tail(
+        d_part, slope * token_coef[None, :], all_rows.T, w_in, m_in, v_in, e_in, weight_out
+    )
     return (
         loss,
         new_w_in,

time: 710 us -> 662 us (0.932)
  Pallas kernels: 0 us -> 364 us
  waiting for transfers between devices: 526 us -> 174 us
  local copies, waits for them, and re-layouts: 62.7 us -> 20.7 us
  matrix products: 41.2 us -> 24.4 us
    pallas_call x0 -> x1, Pallas kernels: none -> 364 us  [backward_tail(): pl.pallas_call(functools.partial(tail_kernel, size, parts), out_shape=(ja...]
    all_gather x4 -> x1, waiting for transfers between devices: 339 us -> 15 us  [gather_rows(): return lax.all_gather(block, axis, axis=0, tiled=True)]
    unnamed x51 -> x34, local copies, waits for them, and re-layouts: 61.7 us -> 19.7 us
    psum x1 -> x0, waiting for transfers between devices: 28.3 us -> none  [on_device(): lax.psum(lax.dot_general(w_out, error, (((1,), (1,)), ((), ())), precisio...]
    dot_general x1 -> x0, matrix products: 12.4 us -> none  [on_device(): lax.dot_general(all_rows, d_hidden, (((0,), (1,)), ((), ())), precision=p...]
  transfers between devices with their start and end apart: 9 -> 5, of which waited for: 9 -> 5; matrix products, arithmetic and copies ran while one was open for 10% -> 0% of each run, Pallas kernels for 0% -> 0%
where the time goes in v3:
time: 662 us; the launch traced here: 661 us
  Pallas kernels  364 us (55%)
  waiting for transfers between devices  174 us (26%)
  blocking collectives  57.5 us (9%)
  matrix products  24.4 us (4%)
  local copies, waits for them, and re-layouts  20.7 us (3%)
  between operations  16.4 us (2%)
    pallas_call x1, Pallas kernels, backward_tail(): pl.pallas_call(functools.partial(tail_kernel, size, parts), out_shape=(ja...  364 us
    reduce_scatter x3, waiting for transfers between devices, scatter_rows(): return lax.psum_scatter(part, axis, scatter_dimension=0, tiled=True)  122 us
    psum x1, waiting for transfers between devices, on_device(): hidden = lax.psum(scatter_rows(hidden_part, 'tok'), 'inp')  36.6 us
    all_gather x3, blocking collectives, gather_rows(): return lax.all_gather(block, axis, axis=0, tiled=True)  32.1 us
    unnamed x34, local copies, waits for them, and re-layouts  19.7 us
    all_gather x1, waiting for transfers between devices, gather_rows(): return lax.all_gather(block, axis, axis=0, tiled=True)  15 us
    all_to_all x1, blocking collectives, on_device(): lax.all_to_all(tokens, 'tok', split_axis=1, concat_axis=0, tiled=True)  13.6 us
  transfers between devices with their start and end apart: 5, of which 5 were waited for; matrix products, arithmetic and copies ran while one was open for 0% of the time, Pallas kernels for 0%

profile of v3, /device:TPU:0, one launch (start us, length us, event | category | flops | bytes accessed | tf_op | source)
XLA Modules:
  0.0 661.2 jit_solution(5718508504485954370)
XLA Ops:
  7.2 0.0 reduce-scatter.4.cloned.1.call-start
  7.2 0.9 copy.39
  8.2 13.6 %all_to_all.19 = f32[32,4,384]{2,0,1:T(8,128)S(1)} all-to-all(f32[32,4,384]{2,0,1:T(8,128)S(1)} %bitcast.29), channel_id=1, replica_groups=mesh['inp'=2,'hid'=4,'tok'=4] {'tok'}, dimensions={1} | all-to-all | bytes 393216 | tf_op jit(solution)/shard_map/all_to_all | solution.py:306
  21.8 0.1 copy.34
  21.9 8.6 %all_gather.15 = f32[512,384]{0,1:T(8,128)S(1)} all-gather(f32[128,384]{0,1:T(8,128)S(1)} %copy.34), channel_id=1, replica_groups=mesh['inp'=2,'hid'=4,'tok'=4] {'hid'}, dimensions={0}, use_global_device_ids=true | all-gather | bytes 983040 | tf_op jit(solution)/shard_map/all_gather | solution.py:64
  30.5 6.0 fusion.35
  36.5 0.0 copy-start.1
  36.5 0.0 reduce-scatter.4.cloned.1.call-update
  36.5 0.0 all-reduce.3.cloned.1.call-start
  36.6 58.8 %reduce-scatter.4.cloned.1.call-done = f32[384,512]{1,0:T(8,128)} async-done(((f32[1536,512]{1,0:T(8,128)}), f32[384,512]{1,0:T(8,128)}) %reduce-scatter.4.cloned.1.call-update) | async-done | bytes 786448 | tf_op jit(solution)/shard_map/reduce_scatter | solution.py:68
  95.3 0.0 all-reduce.3.cloned.1.call-update
  95.4 0.0 reduce-scatter.6.cloned.1.call-start
  95.4 36.6 %all-reduce.3.cloned.1.call-done = f32[384,512]{1,0:T(8,128)} async-done(((f32[384,512]{1,0:T(8,128)}), f32[384,512]{1,0:T(8,128)}) %all-reduce.3.cloned.1.call-update) | async-done | bytes 786448 | tf_op jit(solution)/shard_map/psum | solution.py:309
  132.0 0.0 copy-done.1
  132.0 5.6 fusion.10
  137.6 0.0 copy-start.7
  137.6 0.0 reduce-scatter.6.cloned.1.call-update
  137.7 0.0 copy-start.12
  137.7 0.0 copy-start.11
  137.7 0.0 reduce-scatter.8.cloned.1.call-start
  137.7 38.0 %reduce-scatter.6.cloned.1.call-done = f32[128,1536]{1,0:T(8,128)} async-done(((f32[512,1536]{1,0:T(8,128)}), f32[128,1536]{1,0:T(8,128)}) %reduce-scatter.6.cloned.1.call-update) | async-done | bytes 786448 | tf_op jit(solution)/shard_map/reduce_scatter | solution.py:68
  175.8 0.0 reduce-scatter.8.cloned.1.call-update
  175.8 0.0 all-gather.3.cloned.1.call-start
  175.8 25.5 %reduce-scatter.8.cloned.1.call-done = f32[32,1536]{1,0:T(8,128)} async-done(((f32[128,1536]{1,0:T(8,128)}), f32[32,1536]{1,0:T(8,128)}) %reduce-scatter.8.cloned.1.call-update) | async-done | bytes 196624 | tf_op jit(solution)/shard_map/reduce_scatter | solution.py:68
  201.3 0.0 copy-done.7
  201.3 0.9 sub.22
  202.3 0.0 copy-start.8
  202.3 0.0 copy-start.9
  202.3 0.0 copy-start.10
  202.3 18.4 %all_gather.16 = f32[128,1536]{1,0:T(8,128)} all-gather(f32[32,1536]{1,0:T(8,128)S(1)} %sub.22), channel_id=1, replica_groups=mesh['inp'=2,'hid'=4,'tok'=4] {'tok'}, dimensions={0}, use_global_device_ids=true | all-gather | bytes 983040 | tf_op jit(solution)/shard_map/all_gather | solution.py:64
  220.8 0.0 all-gather.3.cloned.1.call-update
  220.8 0.0 copy-done.12
  220.8 0.6 dynamic-slice
  222.1 0.0 copy-done.11
  222.1 0.2 dynamic-update-slice
  222.3 6.7 %all-reduce = s32[128]{0:T(128)S(1)} all-reduce(s32[128]{0:T(128)S(1)} %dynamic-update-slice), channel_id=1, replica_groups=mesh['inp'=2,'hid'=4,'tok'=4] {'tok'}, use_global_device_ids=true, to_apply=%add | all-reduce | flops 128 | bytes 1024
  229.0 5.0 all-gather
  234.0 0.1 convert_reduce_fusion
  234.1 15.0 %all-gather.3.cloned.1.call-done = f32[512,1536]{1,0:T(8,128)} async-done(((f32[128,1536]{1,0:T(8,128)}), f32[512,1536]{1,0:T(8,128)}) %all-gather.3.cloned.1.call-update) | async-done | bytes 3145744 | tf_op jit(solution)/shard_map/all_gather | solution.py:64
  249.1 2.2 multiply_reduce_fusion
  251.3 0.1 convolution_bitcast_fusion.1
  251.4 5.1 psum.15
  256.6 0.0 copy-done.8
  256.6 0.0 copy-done.9
  256.6 0.0 copy-done.10
  256.6 0.6 multiply_reduce_fusion.1
  257.8 0.1 fusion.11
  258.0 0.0 copy-start.4
  258.0 4.1 convolution_bitcast_fusion.d_part
  262.1 0.0 copy-done.3
  262.1 0.5 fusion.6.scale
  262.6 0.0 copy-done
  262.6 0.0 copy-done.4
  262.6 8.5 %multiply_add_fusion = (f32[384,1536]{1,0:T(8,128)}, f32[384,1536]{1,0:T(8,128)}, f32[384,1536]{1,0:T(8,128)}, f32[384,1536]{1,0:T(8,128)}) fusion(f32[384,1536]{1,0:T(8,128)S(1)} %copy-done.4, f32[384,1536]{1,0:T(8,128)S(1)} %copy-done.1, f32[384,1536]{1,0:T(8,128)} %param.23, f32[384,1536]{1,0:T(8,128)} %param.25, f32[512,1536]{1,0:T(8,128)S(1)} %copy-done, ...), kind=kOutput, calls=%fused_computation.3 | convolution fusion | flops 1823735808 | bytes 22808576 | tf_op jit(solution)/shard_map/dot_general | solution.py:318
  271.0 363.7 %shard_map.205 = (f32[1536,1536]{1,0:T(8,128)}, f32[1536,1536]{1,0:T(8,128)}, f32[384,1536]{1,0:T(8,128)S(1)}, f32[384,1536]{1,0:T(8,128)}, f32[384,1536]{1,0:T(8,128)}) custom-call(f32[384,512]{1,0:T(8,128)S(1)} %convolution_bitcast_fusion.d_part, f32[384,512]{1,0:T(8,128)S(1)} %fusion.6.scale, f32[384,512]{1,0:T(8,128)S(1)} %bitcast.27, f32[384,1536]{1,0:T(8,128)} %w_in.1, ...), custom_call_target="tpu_custom_call" | custom-call | tf_op jit(solution)/shard_map/pallas_call | solution.py:258
  634.8 0.0 copy-start.2
  634.8 8.6 %copy.47 = f32[1536,1536]{1,0:T(8,128)} copy(f32[1536,1536]{1,0:T(8,128)} %get-tuple-element.35) | data formatting | bytes 18874368
  643.4 0.0 copy-done.2
  643.4 3.7 copy.48
  647.1 1.4 copy.49
  648.5 1.1 copy-done.6
  649.7 1.4 copy.50
  651.1 1.1 copy-done.5
  652.2 1.4 copy.51
  (5 shorter events, 0.0 us)
Async XLA Ops:
  7.2 88.2 %reduce-scatter.4.cloned.1.call-start = ((), (), s32[]{:S(2)}) async-start(), calls=%async_computation.4 | async-start | bytes 3932160 | tf_op jit(solution)/shard_map/reduce_scatter | solution.py:68
  36.5 95.6 %copy-start.1 = (f32[384,1536]{1,0:T(8,128)S(1)}, f32[384,1536]{1,0:T(8,128)}, u32[]{:S(2)}) copy-start(f32[384,1536]{1,0:T(8,128)} %param.21) | copy-start | bytes 7077892
  36.5 95.5 %all-reduce.3.cloned.1.call-start = ((), (), s32[]{:S(2)}) async-start(), calls=%async_computation.5 | async-start | bytes 1572864 | tf_op jit(solution)/shard_map/psum | solution.py:309
  95.4 80.4 %reduce-scatter.6.cloned.1.call-start = ((), (), s32[]{:S(2)}) async-start(), calls=%async_computation.6 | async-start | bytes 3932160 | tf_op jit(solution)/shard_map/reduce_scatter | solution.py:68
  137.6 63.7 %copy-start.7 = (f32[32,1536]{1,0:T(8,128)S(1)}, f32[32,1536]{1,0:T(8,128)}, u32[]{:S(2)}) copy-start(f32[32,1536]{1,0:T(8,128)} %param.15) | copy-start | bytes 589828
  137.7 83.1 %copy-start.12 = (u32[32]{0:T(128)S(1)}, u32[32]{0:T(128)}, u32[]{:S(2)}) copy-start(u32[32]{0:T(128)} %constant.56) | copy-start | bytes 388
  137.7 84.4 %copy-start.11 = (s32[32]{0:T(128)S(1)}, s32[32]{0:T(128)}, u32[]{:S(2)}) copy-start(s32[32]{0:T(128)} %param.16) | copy-start | bytes 388
  137.7 63.6 %reduce-scatter.8.cloned.1.call-start = ((), (), s32[]{:S(2)}) async-start(), calls=%async_computation.7 | async-start | bytes 983040 | tf_op jit(solution)/shard_map/reduce_scatter | solution.py:68
  175.8 73.4 %all-gather.3.cloned.1.call-start = ((), (), s32[]{:S(2)}) async-start(), calls=%async_computation.8 | async-start | bytes 3932160 | tf_op jit(solution)/shard_map/all_gather | solution.py:64
  202.3 54.3 %copy-start.8 = (f32[16]{0:T(128)S(1)}, f32[16]{0:T(128)}, u32[]{:S(2)}) copy-start(f32[16]{0:T(128)} %param.19) | copy-start | bytes 196
  202.3 54.3 %copy-start.9 = (f32[16]{0:T(128)S(1)}, f32[16]{0:T(128)}, u32[]{:S(2)}) copy-start(f32[16]{0:T(128)} %param.18) | copy-start | bytes 196
  202.3 54.2 %copy-start.10 = (s32[16]{0:T(128)S(1)}, s32[16]{0:T(128)}, u32[]{:S(2)}) copy-start(s32[16]{0:T(128)} %param.17) | copy-start | bytes 196
  258.0 4.1 copy-start.3
  258.0 4.6 copy-start
  258.0 4.6 copy-start.4
  634.8 8.6 %copy-start.2 = (f32[1536,1536]{1,0:T(8,128)S(1)}, f32[1536,1536]{1,0:T(8,128)}, u32[]{:S(2)}) copy-start(f32[1536,1536]{1,0:T(8,128)} %get-tuple-element.36) | copy-start | bytes 28311556
  647.1 2.5 copy-start.6
  649.6 2.5 copy-start.5
Sparse Core Ops, SparseCore 0:
  36.6 58.6 reduce-scatter.3
  97.6 34.3 all-reduce.2
  137.8 37.9 reduce-scatter.5
  177.9 23.3 reduce-scatter.7
  220.9 28.1 all-gather.2

commit v4 on v3

--- a/solution.py
+++ b/solution.py
@@ -98,11 +98,19 @@
     part_recv,
     line_send,
     line_recv,
+    spread_send,
+    spread_recv,
     own_sem,
 ):
     me = lax.axis_index("tok")
     part = lax.axis_index("inp")
     units, depth = d_part.shape[0], rows_t.shape[0]
+    block = d_part.shape[1] // parts
+
+    def block_of(index):
+        return pl.ds(pl.multiple_of(index * block, block), block)
+
+    my_block = block_of(part)
     mesh_ids = pl.DeviceIdType.MESH
     steps = size - 1
     has_left, has_right = me > 0, me < size - 1
@@ -125,7 +133,7 @@
 
     def part_copy(hop):
         return pltpu.make_async_remote_copy(
-            src_ref=d_part,
+            src_ref=d_part.at[:, block_of(lax.rem(part + hop, parts))],
             dst_ref=others.at[hop - 1],
             send_sem=part_send.at[hop - 1],
             recv_sem=part_recv.at[hop - 1],
@@ -139,6 +147,8 @@
     def line_copy(kind, way, step, shard, own=None):
         array, rows = ((d_all, units), (all_out, units), (all_in, depth))[kind]
         place = array.at[pl.ds(shard * rows, rows)]
+        if kind == 0:
+            place = d_all.at[pl.ds(shard * rows, rows), my_block]
         return pltpu.make_async_remote_copy(
             src_ref=place if own is None else own,
             dst_ref=place,
@@ -148,6 +158,21 @@
             device_id_type=mesh_ids,
         )
 
+    def spread(hop, shard, source):
+        place = d_all.at[pl.ds(shard * units, units), block_of(source)]
+        return pltpu.make_async_remote_copy(
+            src_ref=place,
+            dst_ref=place,
+            send_sem=spread_send.at[hop - 1, shard],
+            recv_sem=spread_recv.at[hop - 1, shard],
+            device_id={"inp": lax.rem(part + hop, parts)},
+            device_id_type=mesh_ids,
+        )
+
+    def start_spread(shard):
+        for hop in range(1, parts):
+            spread(hop, shard, part).start()
+
     def send_own(kind, own):
         @pl.when(has_right)
         def _():
@@ -161,6 +186,8 @@
         @pl.when(me - 1 - step >= 0)
         def _():
             line_copy(kind, 0, step, me - 1 - step).wait_recv()
+            if kind == 0:
+                start_spread(me - 1 - step)
             if step + 1 < steps:
 
                 @pl.when(has_right)
@@ -170,6 +197,8 @@
         @pl.when(me + 1 + step < size)
         def _():
             line_copy(kind, 1, step, me + 1 + step).wait_recv()
+            if kind == 0:
+                start_spread(me + 1 + step)
             if step + 1 < steps:
 
                 @pl.when(has_left)
@@ -197,11 +226,12 @@
     for hop in range(1, parts):
         part_copy(hop).wait_recv()
     mine = pl.ds(me * units, units)
-    total = d_part[...]
+    total = d_part[:, my_block]
     for hop in range(1, parts):
         total = total + others[hop - 1]
-    d_all[mine, :] = total * scale[...]
-    send_own(0, d_all.at[mine])
+    d_all[mine, my_block] = total * scale[:, my_block]
+    send_own(0, d_all.at[mine, my_block])
+    start_spread(me)
 
     early = max(steps - 1, 0)
     for step in range(early):
@@ -209,6 +239,10 @@
     pass_on(1, 0)
     for step in range(early, steps):
         pass_on(0, step)
+
+    for shard in range(size):
+        for hop in range(1, parts):
+            spread(hop, shard, lax.rem(part + parts - hop, parts)).wait_recv()
 
     width = 256
 
@@ -241,6 +275,9 @@
         pass_on(2, step)
     for hop in range(1, parts):
         part_copy(hop).wait_send()
+    for shard in range(size):
+        for hop in range(1, parts):
+            spread(hop, shard, part).wait_send()
     for kind in range(3):
         end_sends(kind)
     own_out.wait()
@@ -267,7 +304,7 @@
         in_specs=[in_vmem] * 7 + [anywhere],
         out_specs=(anywhere, anywhere, in_vmem, in_vmem, in_vmem),
         scratch_shapes=[
-            pltpu.VMEM((hops, units, count), jnp.float32),
+            pltpu.VMEM((hops, units, count // parts), jnp.float32),
             pltpu.VMEM((size * units, count), jnp.float32),
             pltpu.VMEM((depth, wide), jnp.float32),
             pltpu.VMEM((depth, count), jnp.bfloat16),
@@ -276,12 +313,148 @@
             pltpu.SemaphoreType.DMA((hops,)),
             pltpu.SemaphoreType.DMA((3, 2, steps)),
             pltpu.SemaphoreType.DMA((3, 2, steps)),
+            pltpu.SemaphoreType.DMA((hops, size)),
+            pltpu.SemaphoreType.DMA((hops, size)),
             pltpu.SemaphoreType.DMA((2,)),
         ],
         compiler_params=pltpu.CompilerParams(
             collective_id=0, has_side_effects=True, vmem_limit_bytes=48 * 1024 * 1024
         ),
     )(d_part, scale, rows_t, w_in, m_in, v_in, e_in, w_out)
+
+
+def sum_kernel(
+    size,
+    parts,
+    given,
+    result,
+    from_inp,
+    sums,
+    from_tok,
+    whole,
+    inp_send,
+    inp_recv,
+    tok_send,
+    tok_recv,
+    back_send,
+    back_recv,
+):
+    me = lax.axis_index("tok")
+    part = lax.axis_index("inp")
+    rows, block = sums.shape[1:]
+    mesh_ids = pl.DeviceIdType.MESH
+
+    def block_of(index):
+        return pl.ds(pl.multiple_of(index * block, block), block)
+
+    my_block = block_of(part)
+
+    def inp_peer(hop):
+        return lax.rem(part + hop, parts)
+
+    def tok_at(turn):
+        return lax.rem(me + 1 + turn, size)
+
+    def rows_at(turn):
+        return pl.ds(pl.multiple_of(tok_at(turn) * rows, rows), rows)
+
+    barrier = pltpu.get_barrier_semaphore()
+    for hop in range(1, parts):
+        pl.semaphore_signal(
+            barrier, inc=1, device_id={"inp": inp_peer(hop)}, device_id_type=mesh_ids
+        )
+    for turn in range(size - 1):
+        pl.semaphore_signal(
+            barrier, inc=1, device_id={"tok": tok_at(turn)}, device_id_type=mesh_ids
+        )
+    pl.semaphore_wait(barrier, parts - 1 + size - 1)
+
+    def inp_copy(hop, turn):
+        return pltpu.make_async_remote_copy(
+            src_ref=given.at[rows_at(turn), block_of(inp_peer(hop))],
+            dst_ref=from_inp.at[hop - 1, turn],
+            send_sem=inp_send.at[hop - 1, turn],
+            recv_sem=inp_recv.at[hop - 1, turn],
+            device_id={"inp": inp_peer(hop)},
+            device_id_type=mesh_ids,
+        )
+
+    def tok_copy(turn):
+        return pltpu.make_async_remote_copy(
+            src_ref=sums.at[turn],
+            dst_ref=from_tok.at[turn],
+            send_sem=tok_send.at[turn],
+            recv_sem=tok_recv.at[turn],
+            device_id={"tok": tok_at(turn)},
+            device_id_type=mesh_ids,
+        )
+
+    def back_copy(hop, source):
+        place = whole.at[:, block_of(source)]
+        return pltpu.make_async_remote_copy(
+            src_ref=place,
+            dst_ref=place,
+            send_sem=back_send.at[hop - 1],
+            recv_sem=back_recv.at[hop - 1],
+            device_id={"inp": inp_peer(hop)},
+            device_id_type=mesh_ids,
+        )
+
+    for turn in range(size):
+        for hop in range(1, parts):
+            inp_copy(hop, turn).start()
+    for turn in range(size):
+        total = given[rows_at(turn), my_block]
+        for hop in range(1, parts):
+            inp_copy(hop, turn).wait_recv()
+            total = total + from_inp[hop - 1, turn]
+        sums[turn] = total
+        if turn < size - 1:
+            tok_copy(turn).start()
+    total = sums[size - 1]
+    for turn in range(size - 1):
+        tok_copy(turn).wait_recv()
+        total = total + from_tok[turn]
+    whole[:, my_block] = total
+    for hop in range(1, parts):
+        back_copy(hop, part).start()
+    for hop in range(1, parts):
+        back_copy(hop, lax.rem(part + parts - hop, parts)).wait_recv()
+    result[...] = whole[...]
+    for hop in range(1, parts):
+        back_copy(hop, part).wait_send()
+        for turn in range(size):
+            inp_copy(hop, turn).wait_send()
+    for turn in range(size - 1):
+        tok_copy(turn).wait_send()
+
+
+def sum_hidden(given):
+    size, parts = lax.axis_size("tok"), lax.axis_size("inp")
+    rows, count = given.shape[0] // size, given.shape[1]
+    hops, turns, block = max(parts - 1, 1), max(size - 1, 1), count // parts
+    in_vmem = pl.BlockSpec(memory_space=pltpu.VMEM)
+    return pl.pallas_call(
+        functools.partial(sum_kernel, size, parts),
+        out_shape=jax.ShapeDtypeStruct((rows, count), jnp.float32),
+        in_specs=[in_vmem],
+        out_specs=in_vmem,
+        scratch_shapes=[
+            pltpu.VMEM((hops, size, rows, block), jnp.float32),
+            pltpu.VMEM((size, rows, block), jnp.float32),
+            pltpu.VMEM((turns, rows, block), jnp.float32),
+            pltpu.VMEM((rows, count), jnp.float32),
+            pltpu.SemaphoreType.DMA((hops, size)),
+            pltpu.SemaphoreType.DMA((hops, size)),
+            pltpu.SemaphoreType.DMA((turns,)),
+            pltpu.SemaphoreType.DMA((turns,)),
+            pltpu.SemaphoreType.DMA((hops,)),
+            pltpu.SemaphoreType.DMA((hops,)),
+        ],
+        compiler_params=pltpu.CompilerParams(
+            collective_id=1, has_side_effects=True, vmem_limit_bytes=48 * 1024 * 1024
+        ),
+    )(given)
 
 
 def on_device(
@@ -306,10 +479,11 @@
     columns = lax.all_to_all(tokens, "tok", split_axis=1, concat_axis=0, tiled=True)
     all_rows = gather_rows(columns, "hid")
     hidden_part = lax.dot_general(w_in, all_rows, (((0,), (1,)), ((), ())), precision=precise)
-    hidden = lax.psum(scatter_rows(hidden_part, "tok"), "inp")
+    hidden = sum_hidden(hidden_part)
     active, slope = gelu_parts(hidden)
     out_part = contract_rows(active, w_out)
     output = scatter_rows(scatter_rows(out_part, "hid"), "tok")
+    output, onehot, counts = lax.optimization_barrier((output, onehot, counts))
     error = gather_rows(gather_rows(output - targets, "tok"), "hid")
     token_sq = jnp.sum(error * error, axis=1)
     sq_sums = lax.psum(jnp.dot(token_sq, onehot, precision=highest), "inp")

time: 662 us -> 597 us (0.902)
  waiting for transfers between devices: 174 us -> 78.1 us
  Pallas kernels: 364 us -> 394 us
    reduce_scatter x3 -> x2, waiting for transfers between devices: 122 us -> 49.7 us  [scatter_rows(): return lax.psum_scatter(part, axis, scatter_dimension=0, tiled=True)]
    pallas_call x0 -> x1, Pallas kernels: none -> 55.3 us  [sum_hidden(): pl.pallas_call(functools.partial(sum_kernel, size, parts), out_shape=jax....]
    psum x1 -> x0, waiting for transfers between devices: 36.6 us -> none  [on_device(): hidden = lax.psum(scatter_rows(hidden_part, 'tok'), 'inp')]
    pallas_call x1, Pallas kernels: 364 us -> 338 us  [backward_tail(): pl.pallas_call(functools.partial(tail_kernel, size, parts), out_shape=(ja...]
    all_gather x1, waiting for transfers between devices: 15 us -> 28.3 us  [gather_rows(): return lax.all_gather(block, axis, axis=0, tiled=True)]
    unnamed x34 -> x38, local copies, waits for them, and re-layouts: 19.7 us -> 21.3 us
  transfers between devices with their start and end apart: 5 -> 3, of which waited for: 5 -> 3; matrix products, arithmetic and copies ran while one was open for 0% -> 0% of each run, Pallas kernels for 0% -> 0%
where the time goes in v4:
time: 597 us
  Pallas kernels  394 us (66%)
  waiting for transfers between devices  78.1 us (13%)
  blocking collectives  59.1 us (10%)
  local copies, waits for them, and re-layouts  22.4 us (4%)
  matrix products  22.4 us (4%)
  between operations  16.4 us (3%)
    pallas_call x1, Pallas kernels, backward_tail(): pl.pallas_call(functools.partial(tail_kernel, size, parts), out_shape=(ja...  338 us
    pallas_call x1, Pallas kernels, sum_hidden(): pl.pallas_call(functools.partial(sum_kernel, size, parts), out_shape=jax....  55.3 us
    reduce_scatter x2, waiting for transfers between devices, scatter_rows(): return lax.psum_scatter(part, axis, scatter_dimension=0, tiled=True)  49.7 us
    all_gather x3, blocking collectives, gather_rows(): return lax.all_gather(block, axis, axis=0, tiled=True)  32.1 us
    all_gather x1, waiting for transfers between devices, gather_rows(): return lax.all_gather(block, axis, axis=0, tiled=True)  28.3 us
    unnamed x38, local copies, waits for them, and re-layouts  21.3 us
    all_to_all x1, blocking collectives, on_device(): lax.all_to_all(tokens, 'tok', split_axis=1, concat_axis=0, tiled=True)  13.6 us
  transfers between devices with their start and end apart: 3, of which 3 were waited for; matrix products, arithmetic and copies ran while one was open for 0% of the time, Pallas kernels for 0%

profile of v4, /device:TPU:0, one launch (start us, length us, event | category | flops | bytes accessed | tf_op | source)
XLA Modules:
  0.0 596.7 jit_solution(7871561711218675168)
XLA Ops:
  7.2 0.0 reduce-scatter.3.cloned.1.call-start
  7.2 0.9 copy.39
  8.2 13.6 %all_to_all.19 = f32[32,4,384]{2,0,1:T(8,128)S(1)} all-to-all(f32[32,4,384]{2,0,1:T(8,128)S(1)} %bitcast.31), channel_id=1, replica_groups=mesh['inp'=2,'hid'=4,'tok'=4] {'tok'}, dimensions={1} | all-to-all | bytes 393216 | tf_op jit(solution)/shard_map/all_to_all | solution.py:479
  21.8 0.1 copy.34
  21.9 8.6 %all_gather.15 = f32[512,384]{0,1:T(8,128)S(1)} all-gather(f32[128,384]{0,1:T(8,128)S(1)} %copy.34), channel_id=1, replica_groups=mesh['inp'=2,'hid'=4,'tok'=4] {'hid'}, dimensions={0}, use_global_device_ids=true | all-gather | bytes 983040 | tf_op jit(solution)/shard_map/all_gather | solution.py:64
  30.5 4.3 fusion.37.given
  34.8 0.0 copy-start.3
  34.8 55.3 %shard_map.205 = f32[384,512]{1,0:T(8,128)S(1)} custom-call(f32[1536,512]{1,0:T(8,128)S(1)} %fusion.37.given), custom_call_target="tpu_custom_call" | custom-call | tf_op jit(solution)/shard_map/pallas_call | solution.py:437
  90.2 0.0 copy-done.3
  90.2 4.5 fusion.10
  94.6 0.0 copy-start.14
  94.6 0.0 copy-start.13
  94.6 0.0 copy-start.9
  94.6 0.0 reduce-scatter.3.cloned.1.call-update
  94.7 0.0 reduce-scatter.5.cloned.1.call-start
  94.7 39.0 %reduce-scatter.3.cloned.1.call-done = f32[128,1536]{1,0:T(8,128)} async-done(((f32[512,1536]{1,0:T(8,128)}), f32[128,1536]{1,0:T(8,128)}) %reduce-scatter.3.cloned.1.call-update) | async-done | bytes 786448 | tf_op jit(solution)/shard_map/reduce_scatter | solution.py:68
  133.7 0.0 reduce-scatter.5.cloned.1.call-update
  133.7 0.0 all-gather.3.cloned.1.call-start
  133.8 0.0 copy-done.14
  133.8 0.6 dynamic-slice
  135.0 0.0 copy-done.13
  135.0 0.2 dynamic-update-slice
  135.3 8.3 %all-reduce = s32[128]{0:T(128)S(1)} all-reduce(s32[128]{0:T(128)S(1)} %dynamic-update-slice), channel_id=1, replica_groups=mesh['inp'=2,'hid'=4,'tok'=4] {'tok'}, use_global_device_ids=true, to_apply=%add | all-reduce | flops 128 | bytes 1024
  143.5 5.0 all-gather
  148.6 0.1 fusion.12
  148.7 10.7 %reduce-scatter.5.cloned.1.call-done = f32[32,1536]{1,0:T(8,128)} async-done(((f32[128,1536]{1,0:T(8,128)}), f32[32,1536]{1,0:T(8,128)}) %reduce-scatter.5.cloned.1.call-update) | async-done | bytes 196624 | tf_op jit(solution)/shard_map/reduce_scatter | solution.py:68
  159.4 0.0 copy-done.9
  159.4 0.9 sub.22
  160.4 0.0 copy-start.10
  160.4 0.0 copy-start.11
  160.4 0.0 copy-start.12
  160.4 18.5 %all_gather.18 = f32[128,1536]{1,0:T(8,128)} all-gather(f32[32,1536]{1,0:T(8,128)S(1)} %sub.22), channel_id=1, replica_groups=mesh['inp'=2,'hid'=4,'tok'=4] {'tok'}, dimensions={0}, use_global_device_ids=true | all-gather | bytes 983040 | tf_op jit(solution)/shard_map/all_gather | solution.py:64
  178.9 0.0 all-gather.3.cloned.1.call-update
  179.0 28.3 %all-gather.3.cloned.1.call-done = f32[512,1536]{1,0:T(8,128)} async-done(((f32[128,1536]{1,0:T(8,128)}), f32[512,1536]{1,0:T(8,128)}) %all-gather.3.cloned.1.call-update) | async-done | bytes 3145744 | tf_op jit(solution)/shard_map/all_gather | solution.py:64
  207.3 2.2 multiply_reduce_fusion
  209.5 0.1 convolution_bitcast_fusion.1
  209.6 5.1 psum.7
  214.7 0.0 copy-done.10
  214.7 0.0 copy-done.11
  214.7 0.0 copy-done.12
  214.7 0.6 multiply_reduce_fusion.1
  216.0 0.1 fusion.13
  216.1 0.0 copy-start.6
  216.1 0.5 fusion.6.scale
  216.6 0.0 copy-start.2
  216.7 0.0 copy-start.4
  216.7 4.9 convolution_bitcast_fusion.d_part
  221.5 0.0 copy-done.6
  221.5 0.0 copy-done.2
  221.6 0.0 copy-done.4
  221.6 8.5 %multiply_add_fusion = (f32[384,1536]{1,0:T(8,128)}, f32[384,1536]{1,0:T(8,128)}, f32[384,1536]{1,0:T(8,128)}, f32[384,1536]{1,0:T(8,128)}) fusion(f32[384,1536]{1,0:T(8,128)S(1)} %copy-done.6, f32[384,1536]{1,0:T(8,128)S(1)} %copy-done.4, f32[384,1536]{1,0:T(8,128)} %param.23, f32[384,1536]{1,0:T(8,128)} %param.25, f32[512,1536]{1,0:T(8,128)S(1)} %copy-done.2, ...), kind=kOutput, calls=%fused_computation.3 | convolution fusion | flops 1823735808 | bytes 22808576 | tf_op jit(solution)/shard_map/dot_general | solution.py:492
  230.1 338.5 %shard_map.206 = (f32[1536,1536]{1,0:T(8,128)}, f32[1536,1536]{1,0:T(8,128)}, f32[384,1536]{1,0:T(8,128)S(1)}, f32[384,1536]{1,0:T(8,128)}, f32[384,1536]{1,0:T(8,128)}) custom-call(f32[384,512]{1,0:T(8,128)S(1)} %convolution_bitcast_fusion.d_part, f32[384,512]{1,0:T(8,128)S(1)} %fusion.6.scale, f32[384,512]{1,0:T(8,128)S(1)} %bitcast.29, f32[384,1536]{1,0:T(8,128)} %w_in.1, ...), custom_call_target="tpu_custom_call" | custom-call | tf_op jit(solution)/shard_map/pallas_call | solution.py:295
  568.6 0.0 copy-start
  568.6 1.4 copy-done
  570.0 0.0 copy-start.5
  570.0 8.6 %copy.46 = f32[1536,1536]{1,0:T(8,128)} copy(f32[1536,1536]{1,0:T(8,128)} %get-tuple-element.41) | data formatting | bytes 18874368
  578.6 0.0 copy-done.5
  578.6 4.0 copy.47
  582.6 0.0 copy-done.1
  582.6 1.4 copy.48
  584.0 1.1 copy-done.8
  585.1 1.4 copy.49
  586.5 1.1 copy-done.7
  587.6 1.4 copy.50
  (5 shorter events, 0.0 us)
Async XLA Ops:
  7.2 126.5 %reduce-scatter.3.cloned.1.call-start = ((), (), s32[]{:S(2)}) async-start(), calls=%async_computation.3 | async-start | bytes 3932160 | tf_op jit(solution)/shard_map/reduce_scatter | solution.py:68
  34.8 55.3 %copy-start.3 = (f32[384,1536]{1,0:T(8,128)S(1)}, f32[384,1536]{1,0:T(8,128)}, u32[]{:S(2)}) copy-start(f32[384,1536]{1,0:T(8,128)} %param.21) | copy-start | bytes 7077892
  94.6 39.1 %copy-start.14 = (u32[32]{0:T(128)S(1)}, u32[32]{0:T(128)}, u32[]{:S(2)}) copy-start(u32[32]{0:T(128)} %constant.56) | copy-start | bytes 388
  94.6 40.4 %copy-start.13 = (s32[32]{0:T(128)S(1)}, s32[32]{0:T(128)}, u32[]{:S(2)}) copy-start(s32[32]{0:T(128)} %param.16) | copy-start | bytes 388
  94.6 64.8 %copy-start.9 = (f32[32,1536]{1,0:T(8,128)S(1)}, f32[32,1536]{1,0:T(8,128)}, u32[]{:S(2)}) copy-start(f32[32,1536]{1,0:T(8,128)} %param.15) | copy-start | bytes 589828
  94.7 64.8 %reduce-scatter.5.cloned.1.call-start = ((), (), s32[]{:S(2)}) async-start(), calls=%async_computation.4 | async-start | bytes 983040 | tf_op jit(solution)/shard_map/reduce_scatter | solution.py:68
  133.7 73.6 %all-gather.3.cloned.1.call-start = ((), (), s32[]{:S(2)}) async-start(), calls=%async_computation.5 | async-start | bytes 3932160 | tf_op jit(solution)/shard_map/all_gather | solution.py:64
  160.4 54.3 %copy-start.10 = (f32[16]{0:T(128)S(1)}, f32[16]{0:T(128)}, u32[]{:S(2)}) copy-start(f32[16]{0:T(128)} %param.18) | copy-start | bytes 196
  160.4 54.3 %copy-start.11 = (s32[16]{0:T(128)S(1)}, s32[16]{0:T(128)}, u32[]{:S(2)}) copy-start(s32[16]{0:T(128)} %param.17) | copy-start | bytes 196
  160.4 54.3 %copy-start.12 = (f32[16]{0:T(128)S(1)}, f32[16]{0:T(128)}, u32[]{:S(2)}) copy-start(f32[16]{0:T(128)} %param.19) | copy-start | bytes 196
  216.1 5.4 copy-start.6
  216.6 4.9 copy-start.2
  216.7 4.9 copy-start.4
  568.6 1.4 copy-start
  570.0 8.6 %copy-start.5 = (f32[1536,1536]{1,0:T(8,128)S(1)}, f32[1536,1536]{1,0:T(8,128)}, u32[]{:S(2)}) copy-start(f32[1536,1536]{1,0:T(8,128)} %get-tuple-element.42) | copy-start | bytes 28311556
  578.6 4.0 copy-start.1
  582.6 2.5 copy-start.8
  585.1 2.5 copy-start.7
Sparse Core Ops, SparseCore 0:
  94.8 38.8 reduce-scatter.2
  136.1 23.3 reduce-scatter.4
  179.1 28.1 all-gather.2
